TPU v7x, 256 devices: a whole 4x4x8 slice. The times are simulated.
256 devices in a mesh: vocab: 256 (over z, y, x, core).
Axes of the slice: x: 4, y: 4, z: 8, core: 2. Of those that a mesh axis runs over, the one named last changes fastest.
Arguments:
- embedding_table: bfloat16 [65536, 8192], P('vocab'), may hold values from -6 to 6
- token_ids: int32 [32768], P('vocab'), may hold values from 0 to 65535, as said below
- output_grads: bfloat16 [32768, 8192], P('vocab'), may hold values from -6 to 6
Outputs:
- embedded: bfloat16 [32768, 8192], P('vocab')
- table_grads: bfloat16 [65536, 8192], P('vocab')
Inputs may be any that keep to these rules, and one draw needn't show every extreme that they name: `token_ids`: the 128 tokens held by one device have at most 2 ids in any one device's block of consecutive table rows; in every draw one device's block receives exactly 2 ids from the tokens of every device.
All inputs are finite; a program needn't handle non-finite values.
Results may differ from a plain program's by a relative error of at most 0.001.
Values may be sent and summed in bfloat16 or wider, within the bound.
A program may use at most 128 MiB of HBM per device.

v0:
```python
import jax
import jax.numpy as jnp
from jax import lax
from jax.sharding import PartitionSpec as P


def ranks_within(owners):
    count = owners.shape[-1]
    earlier = lax.broadcasted_iota(jnp.int32, (count, count), 1) < lax.broadcasted_iota(
        jnp.int32, (count, count), 0
    )
    same = owners[..., :, None] == owners[..., None, :]
    return jnp.sum((same & earlier).astype(jnp.int32), axis=-1)


def on_device(embedding_table, token_ids, output_grads):
    row_count = embedding_table.shape[0]
    tok_count = token_ids.shape[0]
    width = embedding_table.shape[1]
    devices = lax.axis_size("vocab")
    capacity = 2 * ((tok_count + devices - 1) // devices)
    slots = devices * capacity
    owners = token_ids // row_count
    local_rows = token_ids - owners * row_count
    target = owners * capacity + ranks_within(owners)
    slot_column = lax.broadcasted_iota(jnp.int32, (slots, 1), 0)
    sender = target[None, :] == slot_column
    grad_buffer = jnp.dot(
        sender.astype(jnp.bfloat16), output_grads, preferred_element_type=jnp.float32
    )
    grad_buffer = grad_buffer.astype(jnp.bfloat16).reshape(devices, capacity, width)
    request = jnp.sum(sender.astype(jnp.int32) * (local_rows + 1)[None, :], axis=1)
    received = lax.all_to_all(
        request.reshape(devices, capacity), "vocab", split_axis=0, concat_axis=0, tiled=True
    )
    flat_rows = received.reshape(slots) - 1
    row_iota = lax.broadcasted_iota(jnp.int32, (1, row_count), 1)
    picker = (flat_rows[:, None] == row_iota).astype(jnp.bfloat16)
    picked = jnp.dot(picker, embedding_table, preferred_element_type=jnp.float32)
    picked = picked.astype(jnp.bfloat16).reshape(devices, capacity, width)
    returned = lax.all_to_all(picked, "vocab", split_axis=0, concat_axis=0, tiled=True)
    grads_in = lax.all_to_all(grad_buffer, "vocab", split_axis=0, concat_axis=0, tiled=True)
    slot_row = lax.broadcasted_iota(jnp.int32, (1, slots), 1)
    gatherer = (target[:, None] == slot_row).astype(jnp.bfloat16)
    embedded = jnp.dot(
        gatherer, returned.reshape(slots, width), preferred_element_type=jnp.float32
    ).astype(jnp.bfloat16)
    row_column = lax.broadcasted_iota(jnp.int32, (row_count, 1), 0)
    adder = (row_column == flat_rows[None, :]).astype(jnp.bfloat16)
    table_grads = jnp.dot(
        adder, grads_in.reshape(slots, width), preferred_element_type=jnp.float32
    ).astype(jnp.bfloat16)
    return (embedded, table_grads)


def solution(mesh):
    return jax.shard_map(
        on_device,
        mesh=mesh,
        in_specs=(P("vocab", None), P("vocab"), P("vocab", None)),
        out_specs=(P("vocab", None), P("vocab", None)),
        check_vma=False,
    )
```

profile of v0, /device:TPU:1, one launch (start us, length us, event | category | flops | bytes accessed | tf_op | source)
XLA Modules:
  0.0 451.8 jit_solution(5653080288191876020)
XLA Ops:
  0.6 0.0 copy-start
  0.6 0.8 subtract_add_fusion
  1.5 0.2 convert_reduce_fusion
  1.6 0.2 select_reduce_fusion
  1.8 0.8 all_to_all.12
  2.6 15.7 %all-to-all-start = ((s32[256,1,2]{2,1,0:T(1,128)}), s32[256,1,2]{2,1,0:T(1,128)S(1)}, u32[]{:S(2)}, u32[]{:S(2)}) async-start(s32[256,1,2]{2,1,0:T(1,128)} %bitcast), calls=%async_computation | async-start | bytes 262144 | tf_op jit(solution)/shard_map/all_to_all | solution.py:33
  18.3 0.0 copy-done
  18.3 5.5 %convolution_convert_fusion = bf16[512,8192]{1,0:T(8,128)(2,1)} fusion(bf16[128,8192]{1,0:T(8,128)(2,1)S(1)} %copy-done, s32[128]{0:T(128)S(1)} %multiply_add_fusion), kind=kOutput, calls=%fused_computation | convolution fusion | flops 1078001664 | bytes 10486272 | tf_op jit(solution)/shard_map/dot_general | solution.py:28
  23.8 14.1 %reshape.42 = bf16[256,2,8192]{2,1,0:T(2,128)(2,1)} reshape(bf16[512,8192]{1,0:T(8,128)(2,1)} %convolution_convert_fusion) | data formatting | bytes 16777216 | tf_op jit(solution)/shard_map/reshape | solution.py:31
  37.9 0.0 all-to-all-done
  37.9 14.7 %all-to-all-start.2 = ((bf16[256,2,8192]{2,1,0:T(2,128)(2,1)}), bf16[256,2,8192]{2,1,0:T(2,128)(2,1)}, u32[]{:S(2)}, u32[]{:S(2)}) async-start(bf16[256,2,8192]{2,1,0:T(2,128)(2,1)} %reshape.42), calls=%async_computation.2 | async-start | bytes 16777216 | tf_op jit(solution)/shard_map/all_to_all | solution.py:42
  52.6 0.4 add_reduce_fusion
  53.0 0.1 sub.18
  53.1 7.8 %convolution_convert_fusion.1 = bf16[512,8192]{1,0:T(8,128)(2,1)} fusion(bf16[256,8192]{1,0:T(8,128)(2,1)} %param.3, s32[512]{0:T(512)S(1)} %sub.18), kind=kOutput, calls=%fused_computation.1 | convolution fusion | flops 2151809024 | bytes 12584960 | tf_op jit(solution)/shard_map/dot_general | solution.py:39
  60.9 14.2 %reshape.40 = bf16[256,2,8192]{2,1,0:T(2,128)(2,1)} reshape(bf16[512,8192]{1,0:T(8,128)(2,1)} %convolution_convert_fusion.1) | data formatting | bytes 16777216 | tf_op jit(solution)/shard_map/reshape | solution.py:40
  75.1 163.1 %all-to-all-done.2 = bf16[256,2,8192]{2,1,0:T(2,128)(2,1)} async-done(((bf16[256,2,8192]{2,1,0:T(2,128)(2,1)}), bf16[256,2,8192]{2,1,0:T(2,128)(2,1)}, u32[]{:S(2)}, u32[]{:S(2)}) %all-to-all-start.2) | async-done | bytes 8388640 | tf_op jit(solution)/shard_map/all_to_all | solution.py:42
  238.2 8.9 %all-to-all-start.1 = ((bf16[256,2,8192]{2,1,0:T(2,128)(2,1)}), bf16[256,2,8192]{2,1,0:T(2,128)(2,1)}, u32[]{:S(2)}, u32[]{:S(2)}) async-start(bf16[256,2,8192]{2,1,0:T(2,128)(2,1)} %reshape.40), calls=%async_computation.1 | async-start | bytes 16777216 | tf_op jit(solution)/shard_map/all_to_all | solution.py:41
  247.1 13.1 %reshape.43 = bf16[512,8192]{1,0:T(8,128)(2,1)} reshape(bf16[256,2,8192]{2,1,0:T(2,128)(2,1)} %all-to-all-done.2) | data formatting | bytes 16777216 | tf_op jit(solution)/shard_map/reshape | solution.py:51
  260.2 7.7 %convolution_convert_fusion.2 = bf16[256,8192]{1,0:T(8,128)(2,1)} fusion(bf16[512,8192]{1,0:T(8,128)(2,1)} %reshape.43, s32[512]{0:T(512)S(1)} %sub.18), kind=kOutput, calls=%fused_computation.2 | convolution fusion | flops 2149711872 | bytes 12584960 | tf_op jit(solution)/shard_map/dot_general | solution.py:50
  267.9 164.7 %all-to-all-done.1 = bf16[256,2,8192]{2,1,0:T(2,128)(2,1)} async-done(((bf16[256,2,8192]{2,1,0:T(2,128)(2,1)}), bf16[256,2,8192]{2,1,0:T(2,128)(2,1)}, u32[]{:S(2)}, u32[]{:S(2)}) %all-to-all-start.1) | async-done | bytes 8388640 | tf_op jit(solution)/shard_map/all_to_all | solution.py:41
  432.6 0.0 copy-start.1
  432.6 13.3 %reshape.41 = bf16[512,8192]{1,0:T(8,128)(2,1)} reshape(bf16[256,2,8192]{2,1,0:T(2,128)(2,1)} %all-to-all-done.1) | data formatting | bytes 16777216 | tf_op jit(solution)/shard_map/reshape | solution.py:46
  445.8 6.0 %convolution_convert_fusion.3 = bf16[128,8192]{1,0:T(8,128)(2,1)} fusion(bf16[512,8192]{1,0:T(8,128)(2,1)} %reshape.41, s32[128]{0:T(128)S(1)} %multiply_add_fusion), kind=kOutput, calls=%fused_computation.3 | convolution fusion | flops 1074855936 | bytes 10486272 | tf_op jit(solution)/shard_map/dot_general | solution.py:45
  451.8 0.0 copy-done.1
  (1 shorter events, 0.0 us)
Async XLA Ops:
  0.6 17.6 %copy-start = (bf16[128,8192]{1,0:T(8,128)(2,1)S(1)}, bf16[128,8192]{1,0:T(8,128)(2,1)}, u32[]{:S(2)}) copy-start(bf16[128,8192]{1,0:T(8,128)(2,1)} %param.5) | copy-start | bytes 6291460
  2.6 35.3 %all-to-all-start = ((s32[256,1,2]{2,1,0:T(1,128)}), s32[256,1,2]{2,1,0:T(1,128)S(1)}, u32[]{:S(2)}, u32[]{:S(2)}) async-start(s32[256,1,2]{2,1,0:T(1,128)} %bitcast), calls=%async_computation | async-start | bytes 262144 | tf_op jit(solution)/shard_map/all_to_all | solution.py:33
  37.9 200.2 %all-to-all-start.2 = ((bf16[256,2,8192]{2,1,0:T(2,128)(2,1)}), bf16[256,2,8192]{2,1,0:T(2,128)(2,1)}, u32[]{:S(2)}, u32[]{:S(2)}) async-start(bf16[256,2,8192]{2,1,0:T(2,128)(2,1)} %reshape.42), calls=%async_computation.2 | async-start | bytes 16777216 | tf_op jit(solution)/shard_map/all_to_all | solution.py:42
  238.2 194.4 %all-to-all-start.1 = ((bf16[256,2,8192]{2,1,0:T(2,128)(2,1)}), bf16[256,2,8192]{2,1,0:T(2,128)(2,1)}, u32[]{:S(2)}, u32[]{:S(2)}) async-start(bf16[256,2,8192]{2,1,0:T(2,128)(2,1)} %reshape.40), calls=%async_computation.1 | async-start | bytes 16777216 | tf_op jit(solution)/shard_map/all_to_all | solution.py:41
  432.6 19.2 %copy-start.1 = (bf16[128,8192]{1,0:T(8,128)(2,1)S(1)}, bf16[128,8192]{1,0:T(8,128)(2,1)}, u32[]{:S(2)}) copy-start(bf16[128,8192]{1,0:T(8,128)(2,1)} %param.5) | copy-start | bytes 6291460
where the time goes:
time: 454 us; the launch traced here: 452 us
  waiting for transfers between devices  328 us (72%)
  local copies, waits for them, and re-layouts  55.5 us (12%)
  starting transfers between devices  39.3 us (9%)
  matrix products  27 us (6%)
    all_to_all x1, waiting for transfers between devices, on_device(): lax.all_to_all(picked, 'vocab', split_axis=0, concat_axis=0, tiled=True)  165 us
    all_to_all x1, waiting for transfers between devices, on_device(): lax.all_to_all(grad_buffer, 'vocab', split_axis=0, concat_axis=0, tiled=T...  163 us
    all_to_all x1, starting transfers between devices, on_device(): lax.all_to_all(request.reshape(devices, capacity), 'vocab', split_axis=0,...  15.7 us
    all_to_all x1, starting transfers between devices, on_device(): lax.all_to_all(grad_buffer, 'vocab', split_axis=0, concat_axis=0, tiled=T...  14.7 us
    reshape x1, local copies, waits for them, and re-layouts, on_device(): picked = picked.astype(jnp.bfloat16).reshape(devices, capacity, width)  14.2 us
    reshape x1, local copies, waits for them, and re-layouts, on_device(): grad_buffer.astype(jnp.bfloat16).reshape(devices, capacity, width)  14.1 us
    reshape x1, local copies, waits for them, and re-layouts, on_device(): returned.reshape(slots, width)  13.3 us
    reshape x1, local copies, waits for them, and re-layouts, on_device(): grads_in.reshape(slots, width)  13.1 us
  transfers between devices with their start and end apart: 3, of which 2 were waited for; matrix products, arithmetic and copies ran while one was open for 14% of the time, Pallas kernels for 0%

commit v1 on v0

--- a/solution.py
+++ b/solution.py
@@ -1,7 +1,21 @@
 import jax
 import jax.numpy as jnp
 from jax import lax
+from jax.experimental import pallas as pl
+from jax.experimental.pallas import tpu as pltpu
 from jax.sharding import PartitionSpec as P
+
+MESH = pl.DeviceIdType.MESH
+PLANES = 8
+PEERS = 32
+ROWS = 256
+TOKS = 128
+CAP = 2
+LANE = 128
+POOL = 32
+PAIR = PLANES * CAP
+CHUNKS = 8
+TILE = 512
 
 
 def ranks_within(owners):
@@ -13,7 +27,7 @@
     return jnp.sum((same & earlier).astype(jnp.int32), axis=-1)
 
 
-def on_device(embedding_table, token_ids, output_grads):
+def general(embedding_table, token_ids, output_grads):
     row_count = embedding_table.shape[0]
     tok_count = token_ids.shape[0]
     width = embedding_table.shape[1]
@@ -50,7 +64,304 @@
     table_grads = jnp.dot(
         adder, grads_in.reshape(slots, width), preferred_element_type=jnp.float32
     ).astype(jnp.bfloat16)
-    return (embedded, table_grads)
+    return embedded, table_grads
+
+
+def iota(shape, axis):
+    return lax.broadcasted_iota(jnp.int32, shape, axis)
+
+
+def ones_where(mask):
+    return jnp.where(mask, 1.0, 0.0)
+
+
+def dot(a, b):
+    return jnp.dot(a, b, preferred_element_type=jnp.float32)
+
+
+def dot_nt(a, b):
+    return lax.dot_general(
+        a.astype(jnp.bfloat16),
+        b.astype(jnp.bfloat16),
+        (((1,), (1,)), ((), ())),
+        preferred_element_type=jnp.float32,
+    )
+
+
+def kernel(
+    ids_ref, table_hbm, grads_hbm, emb_hbm, tgr_hbm, flag_ref,
+    table, grads, emb, tgr,
+    z_send, g1_recv, e2_recv,
+    p_send, e1_recv, g2_recv,
+    zreq_send, zreq_recv, preq_send, preq_recv,
+    pack, unpack, spread, unspread, pick, adder,
+    in_sem, out_sem, req_sem,
+    g1_sem, e1_sem, g2_sem, e2_sem,
+):
+    me = lax.axis_index("vocab")
+    z = me // PEERS
+    p = lax.rem(me, PEERS)
+    width = table.shape[2]
+
+    def z_peer(j):
+        return lax.rem(z + j, PLANES)
+
+    def p_peer(j):
+        return lax.rem(p + j, PEERS)
+
+    def loop(lo, hi, body):
+        def step(j, carry):
+            body(j)
+            return carry
+
+        lax.fori_loop(lo, hi, step, 0)
+
+    def columns(k):
+        return pl.ds(pl.multiple_of(k * width, width), width)
+
+    def grads_in(k):
+        return pltpu.make_async_copy(grads_hbm.at[:, columns(k)], grads.at[k], in_sem.at[0, k])
+
+    def table_in(k):
+        return pltpu.make_async_copy(table_hbm.at[:, columns(k)], table.at[k], in_sem.at[1, k])
+
+    loop(0, CHUNKS, lambda k: grads_in(k).start())
+    loop(0, CHUNKS, lambda k: table_in(k).start())
+
+    barrier = pltpu.get_barrier_semaphore()
+
+    def greet(device):
+        pl.semaphore_signal(barrier, inc=1, device_id=(device,), device_id_type=MESH)
+
+    loop(1, PLANES, lambda j: greet(z_peer(j) * PEERS + p))
+    loop(1, PEERS, lambda j: greet(z * PEERS + p_peer(j)))
+
+    def z_start(src, dst, send, recv, own):
+        def one(j):
+            t = z_peer(j)
+            pltpu.make_async_remote_copy(
+                src_ref=src.at[t], dst_ref=dst.at[z], send_sem=send, recv_sem=recv,
+                device_id=(t * PEERS + p,), device_id_type=MESH,
+            ).start()
+
+        loop(1, PLANES, one)
+        pltpu.make_async_copy(src.at[z], dst.at[z], own).start()
+
+    def p_start(src, dst, send, recv, own):
+        def one(j):
+            t = p_peer(j)
+            pltpu.make_async_remote_copy(
+                src_ref=src.at[t], dst_ref=dst.at[p], send_sem=send, recv_sem=recv,
+                device_id=(z * PEERS + t,), device_id_type=MESH,
+            ).start()
+
+        loop(1, PEERS, one)
+        pltpu.make_async_copy(src.at[p], dst.at[p], own).start()
+
+    def wait_bytes(ref, count, sem):
+        pltpu.make_async_copy(ref.at[pl.ds(0, count)], ref.at[pl.ds(0, count)], sem).wait()
+
+    def wait_recv(dst, count, recv, own):
+        wait_bytes(dst, count - 1, recv)
+        wait_bytes(dst, 1, own)
+
+    ids = ids_ref[...]
+    plane = lax.shift_right_logical(ids, 13)
+    owner = lax.shift_right_logical(ids, 8)
+    earlier = iota((TOKS, TOKS), 0) < iota((TOKS, TOKS), 1)
+
+    def rank(key):
+        row = jnp.broadcast_to(key.astype(jnp.float32), (TOKS, TOKS))
+        return jnp.sum(ones_where((row == row.T) & earlier), axis=0, keepdims=True).astype(jnp.int32)
+
+    place = rank(plane)
+    twin = rank(owner)
+    late = ones_where(jnp.max(place, axis=1, keepdims=True) >= POOL)
+    slot = jnp.where(place < POOL, plane * POOL + place, -1)
+    packer = ones_where(iota((PLANES * POOL, TOKS), 0) == slot)
+    pack[...] = packer.astype(jnp.bfloat16)
+    unpack[...] = packer.T.astype(jnp.bfloat16)
+    row_code = ((ids & (ROWS - 1)) + 1).astype(jnp.float32)
+    pair_code = ((owner & (PEERS - 1)) * CAP + twin).astype(jnp.float32)
+    line = iota((PLANES * 8, TOKS), 0)
+    part = line & 7
+    fields = jnp.where(part == 0, row_code, jnp.where(part == 1, pair_code, 0.0))
+    fields = jnp.where((line >> 3) == plane, fields, 0.0)
+    lane_at = jnp.where(place < POOL, lax.rem(z, 4) * POOL + place, -1)
+    where_at = ones_where(iota((LANE, TOKS), 0) == lane_at)
+    message = dot_nt(fields, where_at) + jnp.where(iota((PLANES * 8, LANE), 0) & 7 == 2, late, 0.0)
+    zreq_send[...] = message.reshape(PLANES, 8, LANE)
+
+    pl.semaphore_wait(barrier, PLANES - 1 + PEERS - 1)
+    z_start(zreq_send, zreq_recv, req_sem.at[0], req_sem.at[1], req_sem.at[2])
+
+    def pack_grads(k):
+        grads_in(k).wait()
+        for c in range(0, width, TILE):
+            out = dot(pack[...], grads[k, :, c : c + TILE]).astype(jnp.bfloat16)
+            z_send[k, :, :, c : c + TILE] = out.reshape(PLANES, POOL, TILE)
+        z_start(z_send.at[k], g1_recv.at[k], g1_sem.at[0, k], g1_sem.at[1, k], g1_sem.at[2, k])
+
+    pack_grads(0)
+
+    wait_recv(zreq_recv, PLANES, req_sem.at[1], req_sem.at[2])
+    got = zreq_recv[...]
+    got = jnp.concatenate([got[:4].sum(axis=0), got[4:].sum(axis=0)], axis=1)
+    entries = PLANES * POOL
+    entry_row = got[0:1, :]
+    entry_pair = got[1:2, :].astype(jnp.int32)
+    late = jnp.sum(got[2:3, :], axis=1, keepdims=True)
+    valid = entry_row > 0.0
+    entry_peer = entry_pair >> 1
+    entry_slot = (iota((1, entries), 1) >> 5) * CAP + (entry_pair & 1)
+    pair_slot = jnp.where(valid, entry_peer * PAIR + entry_slot, -1)
+    line = iota((PEERS * 8, entries), 0)
+    fields = jnp.where(((line & 7) == 0) & ((line >> 3) == entry_peer), entry_row, 0.0)
+    lane_at = jnp.where(valid, lax.rem(p, 8) * PAIR + entry_slot, -1)
+    where_at = ones_where(iota((LANE, entries), 0) == lane_at)
+    message = dot_nt(fields, where_at) + jnp.where(iota((PEERS * 8, LANE), 0) & 7 == 2, late, 0.0)
+    preq_send[...] = message.reshape(PEERS, 8, LANE)
+    p_start(preq_send, preq_recv, req_sem.at[3], req_sem.at[4], req_sem.at[5])
+    spreader = ones_where(iota((PEERS * PAIR, entries), 0) == pair_slot)
+    spread[...] = spreader.astype(jnp.bfloat16)
+    unspread[...] = spreader.T.astype(jnp.bfloat16)
+
+    wait_recv(preq_recv, PEERS, req_sem.at[4], req_sem.at[5])
+    got = preq_recv[...]
+    got = jnp.concatenate([got[8 * g : 8 * g + 8].sum(axis=0) for g in range(4)], axis=1)
+    wanted = got[0:1, :]
+    flag_ref[...] = jnp.broadcast_to(jnp.sum(got[2:3, :], axis=1, keepdims=True), flag_ref.shape)
+    adding = ones_where((iota((ROWS, PEERS * PAIR), 0) + 1).astype(jnp.float32) == wanted)
+    adder[...] = adding.astype(jnp.bfloat16)
+    pick[...] = adding.T.astype(jnp.bfloat16)
+
+    def pick_rows(k):
+        table_in(k).wait()
+        for c in range(0, width, TILE):
+            out = dot(pick[...], table[k, :, c : c + TILE]).astype(jnp.bfloat16)
+            p_send[k, :, :, c : c + TILE] = out.reshape(PEERS, PAIR, TILE)
+        p_start(p_send.at[k], e1_recv.at[k], e1_sem.at[0, k], e1_sem.at[1, k], e1_sem.at[2, k])
+
+    pick_rows(0)
+
+    def first_hop(k):
+        pack_grads(k)
+        pick_rows(k)
+
+    loop(1, CHUNKS, first_hop)
+
+    def second_hop(k):
+        wait_recv(e1_recv.at[k], PEERS, e1_sem.at[1, k], e1_sem.at[2, k])
+        wait_bytes(z_send.at[k], PLANES - 1, g1_sem.at[0, k])
+        wait_recv(g1_recv.at[k], PLANES, g1_sem.at[1, k], g1_sem.at[2, k])
+        for c in range(0, width, TILE):
+            rows = e1_recv[k, :, :, c : c + TILE].reshape(PEERS * PAIR, TILE)
+            out = dot(unspread[...], rows).astype(jnp.bfloat16)
+            z_send[k, :, :, c : c + TILE] = out.reshape(PLANES, POOL, TILE)
+        z_start(z_send.at[k], e2_recv.at[k], e2_sem.at[0, k], e2_sem.at[1, k], e2_sem.at[2, k])
+        wait_bytes(p_send.at[k], PEERS - 1, e1_sem.at[0, k])
+        for c in range(0, width, TILE):
+            rows = g1_recv[k, :, :, c : c + TILE].reshape(entries, TILE)
+            out = dot(spread[...], rows).astype(jnp.bfloat16)
+            p_send[k, :, :, c : c + TILE] = out.reshape(PEERS, PAIR, TILE)
+        p_start(p_send.at[k], g2_recv.at[k], g2_sem.at[0, k], g2_sem.at[1, k], g2_sem.at[2, k])
+
+    loop(0, CHUNKS, second_hop)
+
+    def emb_out(k):
+        return pltpu.make_async_copy(emb.at[k], emb_hbm.at[:, columns(k)], out_sem.at[0, k])
+
+    def tgr_out(k):
+        return pltpu.make_async_copy(tgr.at[k], tgr_hbm.at[:, columns(k)], out_sem.at[1, k])
+
+    def finish(k):
+        wait_recv(e2_recv.at[k], PLANES, e2_sem.at[1, k], e2_sem.at[2, k])
+        for c in range(0, width, TILE):
+            rows = e2_recv[k, :, :, c : c + TILE].reshape(entries, TILE)
+            emb[k, :, c : c + TILE] = dot(unpack[...], rows).astype(jnp.bfloat16)
+        emb_out(k).start()
+        wait_recv(g2_recv.at[k], PEERS, g2_sem.at[1, k], g2_sem.at[2, k])
+        for c in range(0, width, TILE):
+            rows = g2_recv[k, :, :, c : c + TILE].reshape(PEERS * PAIR, TILE)
+            tgr[k, :, c : c + TILE] = dot(adder[...], rows).astype(jnp.bfloat16)
+        tgr_out(k).start()
+
+    loop(0, CHUNKS, finish)
+
+    def drain(k):
+        emb_out(k).wait()
+        tgr_out(k).wait()
+        wait_bytes(z_send.at[k], PLANES - 1, e2_sem.at[0, k])
+        wait_bytes(p_send.at[k], PEERS - 1, g2_sem.at[0, k])
+
+    loop(0, CHUNKS, drain)
+    wait_bytes(zreq_send, PLANES - 1, req_sem.at[0])
+    wait_bytes(preq_send, PEERS - 1, req_sem.at[3])
+
+
+def routed(embedding_table, token_ids, output_grads):
+    depth = embedding_table.shape[1]
+    width = depth // CHUNKS
+    entries, slots = PLANES * POOL, PEERS * PAIR
+    bf16, f32 = jnp.bfloat16, jnp.float32
+    anywhere = pl.BlockSpec(memory_space=pl.ANY)
+    vmem = pl.BlockSpec(memory_space=pltpu.VMEM)
+    dma = pltpu.SemaphoreType.DMA
+    return pl.pallas_call(
+        kernel,
+        out_shape=(
+            jax.ShapeDtypeStruct((TOKS, depth), bf16),
+            jax.ShapeDtypeStruct((ROWS, depth), bf16),
+            jax.ShapeDtypeStruct((8, LANE), f32),
+        ),
+        in_specs=[vmem, anywhere, anywhere],
+        out_specs=(anywhere, anywhere, vmem),
+        scratch_shapes=[
+            pltpu.VMEM((CHUNKS, ROWS, width), bf16),
+            pltpu.VMEM((CHUNKS, TOKS, width), bf16),
+            pltpu.VMEM((CHUNKS, TOKS, width), bf16),
+            pltpu.VMEM((CHUNKS, ROWS, width), bf16),
+            pltpu.VMEM((CHUNKS, PLANES, POOL, width), bf16),
+            pltpu.VMEM((CHUNKS, PLANES, POOL, width), bf16),
+            pltpu.VMEM((CHUNKS, PLANES, POOL, width), bf16),
+            pltpu.VMEM((CHUNKS, PEERS, PAIR, width), bf16),
+            pltpu.VMEM((CHUNKS, PEERS, PAIR, width), bf16),
+            pltpu.VMEM((CHUNKS, PEERS, PAIR, width), bf16),
+            pltpu.VMEM((PLANES, 8, LANE), f32),
+            pltpu.VMEM((PLANES, 8, LANE), f32),
+            pltpu.VMEM((PEERS, 8, LANE), f32),
+            pltpu.VMEM((PEERS, 8, LANE), f32),
+            pltpu.VMEM((entries, TOKS), bf16),
+            pltpu.VMEM((TOKS, entries), bf16),
+            pltpu.VMEM((slots, entries), bf16),
+            pltpu.VMEM((entries, slots), bf16),
+            pltpu.VMEM((slots, ROWS), bf16),
+            pltpu.VMEM((ROWS, slots), bf16),
+            dma((2, CHUNKS)),
+            dma((2, CHUNKS)),
+            dma((6,)),
+            dma((3, CHUNKS)),
+            dma((3, CHUNKS)),
+            dma((3, CHUNKS)),
+            dma((3, CHUNKS)),
+        ],
+        compiler_params=pltpu.CompilerParams(
+            collective_id=0, has_side_effects=True, vmem_limit_bytes=56 * 1024 * 1024
+        ),
+    )(token_ids.reshape(1, TOKS), embedding_table, output_grads)
+
+
+def on_device(embedding_table, token_ids, output_grads):
+    embedded, table_grads, late = routed(embedding_table, token_ids, output_grads)
+
+    def again(_):
+        emb, tgr = general(embedding_table, token_ids, output_grads)
+        return emb, tgr, jnp.float32(0)
+
+    embedded, table_grads, _ = lax.while_loop(
+        lambda held: held[2] > 0, again, (embedded, table_grads, late[0, 0])
+    )
+    return embedded, table_grads
 
 
 def solution(mesh):

time: 454 us -> 223 us (0.49)
  waiting for transfers between devices: 328 us -> 0 us
  Pallas kernels: 0 us -> 211 us
  local copies, waits for them, and re-layouts: 55.5 us -> 6.46 us
  starting transfers between devices: 39.3 us -> 0 us
  matrix products: 27 us -> 0 us
    all_to_all x3 -> x0, waiting for transfers between devices: 328 us -> none  [the longest x1 165 us: on_device(): lax.all_to_all(picked, 'vocab', split_axis=0, concat_axis=0, tiled=True)]
    pallas_call x0 -> x1, Pallas kernels: none -> 211 us  [routed(): pl.pallas_call(kernel, out_shape=(jax.ShapeDtypeStruct((TOKS, depth), bf1...]
    reshape x4 -> x0, local copies, waits for them, and re-layouts: 54.6 us -> none  [the longest x1 14.2 us: on_device(): picked = picked.astype(jnp.bfloat16).reshape(devices, capacity, width)]
    all_to_all x3 -> x0, starting transfers between devices: 39.3 us -> none  [the longest x1 15.7 us: on_device(): lax.all_to_all(request.reshape(devices, capacity), 'vocab', split_axis=0,...]
    dot_general x4 -> x0, matrix products: 27 us -> none  [the longest x1 7.78 us: on_device(): jnp.dot(picker, embedding_table, preferred_element_type=jnp.float32)]
    unnamed x4 -> x8, local copies, waits for them, and re-layouts: 0.02 us -> 5.27 us
  transfers between devices with their start and end apart: 3 -> 0, of which waited for: 2 -> 0; matrix products, arithmetic and copies ran while one was open for 14% -> 0% of each run, Pallas kernels for 0% -> 0%
where the time goes in v1:
time: 223 us; the launch traced here: 219 us
  Pallas kernels  211 us (95%)
  local copies, waits for them, and re-layouts  6.46 us (3%)
    pallas_call x1, Pallas kernels, routed(): pl.pallas_call(kernel, out_shape=(jax.ShapeDtypeStruct((TOKS, depth), bf1...  211 us
    unnamed x8, local copies, waits for them, and re-layouts  5.27 us

profile of v1, /device:TPU:1, one launch (start us, length us, event | category | flops | bytes accessed | tf_op | source)
XLA Modules:
  0.0 218.9 jit_solution(8363090894103202787)
XLA Ops:
  0.6 0.0 copy-start.2
  0.6 0.0 copy-start
  0.6 210.9 %shard_map.50 = (bf16[128,8192]{1,0:T(8,128)(2,1)}, bf16[256,8192]{1,0:T(8,128)(2,1)}, f32[8,128]{1,0:T(8,128)}) custom-call(s32[1,128]{1,0:T(1,128)} %bitcast.7, bf16[256,8192]{1,0:T(8,128)(2,1)} %table_hbm.1, bf16[128,8192]{1,0:T(8,128)(2,1)} %grads_hbm.1), custom_call_target="tpu_custom_call" | custom-call | tf_op jit(solution)/shard_map/pallas_call | solution.py:310
  211.6 1.2 slice.3
  212.8 0.0 copy-done.2
  212.8 0.0 copy-done
  212.8 0.9 while.11
  213.7 0.0 copy-start.1
  213.7 3.2 %copy.20 = bf16[128,8192]{1,0:T(8,128)(2,1)} copy(bf16[128,8192]{1,0:T(8,128)(2,1)} %get-tuple-element.80) | data formatting | bytes 4194304
  216.9 0.0 copy-done.1
  216.9 2.0 copy.21
Async XLA Ops:
  0.6 212.1 %copy-start.2 = (s32[128]{0:T(128)S(1)}, s32[128]{0:T(128)}, u32[]{:S(2)}) copy-start(s32[128]{0:T(128)} %param.6) | copy-start | bytes 1540
  0.6 212.1 %copy-start = (bf16[128,8192]{1,0:T(8,128)(2,1)S(1)}, bf16[128,8192]{1,0:T(8,128)(2,1)}, u32[]{:S(2)}) copy-start(bf16[128,8192]{1,0:T(8,128)(2,1)} %grads_hbm.1) | copy-start | bytes 6291460
  213.7 3.3 %copy-start.1 = (bf16[256,8192]{1,0:T(8,128)(2,1)S(1)}, bf16[256,8192]{1,0:T(8,128)(2,1)}, u32[]{:S(2)}) copy-start(bf16[256,8192]{1,0:T(8,128)(2,1)} %get-tuple-element.81) | copy-start | bytes 12582916

commit v2 on v0

--- a/solution.py
+++ b/solution.py
@@ -1,7 +1,23 @@
 import jax
 import jax.numpy as jnp
 from jax import lax
+from jax.experimental import pallas as pl
+from jax.experimental.pallas import tpu as pltpu
 from jax.sharding import PartitionSpec as P
+
+MESH = pl.DeviceIdType.MESH
+PLANES = 8
+CHIPS = 16
+CORES = 2
+ROWS = 256
+TOKS = 128
+LANE = 128
+POOL = 56
+STRIDE = 64
+PAIR = 48
+CHUNKS = 4
+ENTRIES = PLANES * STRIDE
+SLOTS = CHIPS * PAIR
 
 
 def ranks_within(owners):
@@ -13,7 +29,7 @@
     return jnp.sum((same & earlier).astype(jnp.int32), axis=-1)
 
 
-def on_device(embedding_table, token_ids, output_grads):
+def general(embedding_table, token_ids, output_grads):
     row_count = embedding_table.shape[0]
     tok_count = token_ids.shape[0]
     width = embedding_table.shape[1]
@@ -50,7 +66,354 @@
     table_grads = jnp.dot(
         adder, grads_in.reshape(slots, width), preferred_element_type=jnp.float32
     ).astype(jnp.bfloat16)
-    return (embedded, table_grads)
+    return embedded, table_grads
+
+
+def iota(shape, axis):
+    return lax.broadcasted_iota(jnp.int32, shape, axis)
+
+
+def ones_where(mask):
+    return jnp.where(mask, 1.0, 0.0)
+
+
+def dot(a, b):
+    return jnp.dot(a, b, preferred_element_type=jnp.float32)
+
+
+def dot_nt(a, b):
+    return lax.dot_general(
+        a.astype(jnp.bfloat16),
+        b.astype(jnp.bfloat16),
+        (((1,), (1,)), ((), ())),
+        preferred_element_type=jnp.float32,
+    )
+
+
+def kernel(
+    ids_ref, table_hbm, grads_hbm, emb_hbm, tgr_hbm, flag_ref,
+    table, grads, emb, tgr,
+    z_send, g1_recv, e2_recv,
+    p_send, e1_recv, g2_recv,
+    ids_send, ids_recv, zreq_send, zreq_recv, preq_send, preq_recv, flag_send, flag_recv,
+    pack, unpack, spread, unspread, pick, adder,
+    in_sem, out_sem, mate_sem, late_sem, req_sem,
+    g1_sem, e1_sem, g2_sem, e2_sem,
+):
+    me = lax.axis_index("vocab")
+    core = lax.rem(me, CORES)
+    mate = 1 - core
+    z = me // (CHIPS * CORES)
+    p = lax.rem(me // CORES, CHIPS)
+    width = table.shape[3]
+    half = width // 2
+    bf16 = jnp.bfloat16
+
+    def device(plane, chip, which):
+        return ((plane * CHIPS + chip) * CORES + which,)
+
+    def z_peer(j):
+        return lax.rem(z + j, PLANES)
+
+    def p_peer(j):
+        return lax.rem(p + j, CHIPS)
+
+    def loop(lo, hi, body):
+        def step(j, carry):
+            body(j)
+            return carry
+
+        lax.fori_loop(lo, hi, step, 0)
+
+    def columns(which, k):
+        return pl.ds(pl.multiple_of((which * CHUNKS + k) * width, width), width)
+
+    def own_in(hbm, vmem, i, k):
+        return pltpu.make_async_copy(hbm.at[:, columns(core, k)], vmem.at[k, core], in_sem.at[i, k])
+
+    def mate_in(hbm, vmem, i, k):
+        return pltpu.make_async_remote_copy(
+            src_ref=hbm.at[:, columns(mate, k)], dst_ref=vmem.at[k, core],
+            send_sem=mate_sem.at[i, k], recv_sem=mate_sem.at[i + 1, k],
+            device_id=device(z, p, mate), device_id_type=MESH,
+        )
+
+    loop(0, CHUNKS, lambda k: own_in(grads_hbm, grads, 0, k).start())
+    loop(0, CHUNKS, lambda k: own_in(table_hbm, table, 1, k).start())
+
+    barrier = pltpu.get_barrier_semaphore()
+
+    def greet(plane, chip, which):
+        pl.semaphore_signal(barrier, inc=1, device_id=device(plane, chip, which), device_id_type=MESH)
+
+    greet(z, p, mate)
+    loop(1, PLANES, lambda j: greet(z_peer(j), p, core))
+    loop(1, CHIPS, lambda j: greet(z, p_peer(j), core))
+
+    def z_start(src, dst, send, recv, own):
+        def one(j):
+            t = z_peer(j)
+            pltpu.make_async_remote_copy(
+                src_ref=src.at[t], dst_ref=dst.at[z], send_sem=send, recv_sem=recv,
+                device_id=device(t, p, core), device_id_type=MESH,
+            ).start()
+
+        loop(1, PLANES, one)
+        pltpu.make_async_copy(src.at[z], dst.at[z], own).start()
+
+    def p_start(src, dst, send, recv, own):
+        def one(j):
+            t = p_peer(j)
+            pltpu.make_async_remote_copy(
+                src_ref=src.at[t], dst_ref=dst.at[p], send_sem=send, recv_sem=recv,
+                device_id=device(z, t, core), device_id_type=MESH,
+            ).start()
+
+        loop(1, CHIPS, one)
+        pltpu.make_async_copy(src.at[p], dst.at[p], own).start()
+
+    def wait_bytes(ref, count, sem):
+        pltpu.make_async_copy(ref.at[pl.ds(0, count)], ref.at[pl.ds(0, count)], sem).wait()
+
+    def wait_recv(dst, count, recv, own):
+        wait_bytes(dst, count - 1, recv)
+        wait_bytes(dst, 1, own)
+
+    ids_send[...] = jnp.broadcast_to(ids_ref[...], ids_send.shape)
+    ids_recv[core] = ids_send[...]
+    pl.semaphore_wait(barrier, 1 + PLANES - 1 + CHIPS - 1)
+    ids_copy = pltpu.make_async_remote_copy(
+        src_ref=ids_send, dst_ref=ids_recv.at[core], send_sem=req_sem.at[0], recv_sem=req_sem.at[1],
+        device_id=device(z, p, mate), device_id_type=MESH,
+    )
+    ids_copy.start()
+    loop(0, CHUNKS, lambda k: mate_in(grads_hbm, grads, 0, k).start())
+    loop(0, CHUNKS, lambda k: mate_in(table_hbm, table, 2, k).start())
+    ids_copy.wait()
+    got = ids_recv[...]
+    ids = jnp.concatenate([got[0, 0:1], got[1, 0:1]], axis=1)
+    toks = CORES * TOKS
+
+    def ranks(keys, kinds, count):
+        same = ones_where(iota((kinds, count), 0) == keys)
+        earlier = ones_where(iota((count, count), 0) < iota((count, count), 1))
+        before = dot(same.astype(bf16), earlier.astype(bf16))
+        return jnp.sum(same * before, axis=0, keepdims=True).astype(jnp.int32)
+
+    plane = lax.shift_right_logical(ids, 13)
+    owner = lax.shift_right_logical(ids, 8)
+    place = ranks(plane, PLANES, toks)
+    late = ones_where(jnp.max(place, axis=1, keepdims=True) >= POOL)
+    fits = place < POOL
+    packer = ones_where(iota((ENTRIES, toks), 0) == jnp.where(fits, plane * STRIDE + place, -1))
+    pack[...] = packer.astype(bf16)
+    row_code = ((ids & (ROWS - 1)) + 1).astype(jnp.float32)
+    owner_code = (owner & (CHIPS * CORES - 1)).astype(jnp.float32)
+    line = iota((PLANES * 8, toks), 0)
+    part = line & 7
+    fields = jnp.where(part == 0, row_code, jnp.where(part == 1, owner_code, 0.0))
+    fields = jnp.where((line >> 3) == plane, fields, 0.0)
+    lane_at = jnp.where(fits, lax.rem(z, 2) * STRIDE + place, -1)
+    where_at = ones_where(iota((LANE, toks), 0) == lane_at)
+    message = dot_nt(fields, where_at) + jnp.where(iota((PLANES * 8, LANE), 0) & 7 == 2, late, 0.0)
+    zreq_send[...] = message.reshape(PLANES, 8, LANE)
+    z_start(zreq_send, zreq_recv, req_sem.at[2], req_sem.at[3], req_sem.at[4])
+
+    def store_z(k, matrix, rows):
+        parts = []
+        for h in range(2):
+            out = dot(matrix, rows[:, h * half : (h + 1) * half])
+            parts.append(out.reshape(PLANES, STRIDE, half)[:, :POOL])
+        z_send[k] = jnp.concatenate(parts, axis=1).astype(bf16)
+
+    def load_z(ref, k, h):
+        rows = ref[k].astype(jnp.float32)[:, h * POOL : (h + 1) * POOL]
+        rows = jnp.concatenate([rows, jnp.zeros((PLANES, STRIDE - POOL, half), jnp.float32)], axis=1)
+        return rows.reshape(ENTRIES, half).astype(bf16)
+
+    def pack_grads(k):
+        own_in(grads_hbm, grads, 0, k).wait()
+        mate_in(grads_hbm, grads, 0, k).wait_recv()
+        store_z(k, pack[...], grads[k].reshape(toks, width))
+        z_start(z_send.at[k], g1_recv.at[k], g1_sem.at[0, k], g1_sem.at[1, k], g1_sem.at[2, k])
+
+    pack_grads(0)
+    unpack[...] = packer.T.astype(bf16)
+
+    wait_recv(zreq_recv, PLANES, req_sem.at[3], req_sem.at[4])
+    got = zreq_recv[...]
+    got = jnp.concatenate([got[2 * g] + got[2 * g + 1] for g in range(PLANES // 2)], axis=1)
+    entry_row = got[0:1]
+    entry_owner = got[1:2].astype(jnp.int32)
+    valid = entry_row > 0.0
+    entry_chip = jnp.where(valid, entry_owner >> 1, -1)
+    entry_core = (entry_owner & 1).astype(jnp.float32)
+    place = ranks(entry_chip, CHIPS, ENTRIES)
+    late = jnp.sum(got[2:3], axis=1, keepdims=True)
+    late = late + ones_where(jnp.max(place, axis=1, keepdims=True) >= PAIR)
+    fits = valid & (place < PAIR)
+    line = iota((CHIPS * 8, ENTRIES), 0)
+    part = line & 7
+    fields = jnp.where(part == 0, entry_row, jnp.where(part == 1, entry_core, 0.0))
+    fields = jnp.where((line >> 3) == entry_chip, fields, 0.0)
+    lanes = CHIPS // 2 * PAIR
+    lane_at = jnp.where(fits, lax.rem(p, CHIPS // 2) * PAIR + place, -1)
+    where_at = ones_where(iota((lanes, ENTRIES), 0) == lane_at)
+    message = dot_nt(fields, where_at) + jnp.where(iota((CHIPS * 8, lanes), 0) & 7 == 2, late, 0.0)
+    preq_send[...] = message.reshape(CHIPS, 8, lanes)
+    p_start(preq_send, preq_recv, req_sem.at[5], req_sem.at[6], req_sem.at[7])
+    spreader = ones_where(iota((SLOTS, ENTRIES), 0) == jnp.where(fits, entry_chip * PAIR + place, -1))
+    spread[...] = spreader.astype(bf16)
+    unspread[...] = spreader.T.astype(bf16)
+
+    wait_recv(preq_recv, CHIPS, req_sem.at[6], req_sem.at[7])
+    got = preq_recv[...]
+    got = jnp.concatenate([got[:8].sum(axis=0), got[8:].sum(axis=0)], axis=1)
+    wanted = got[0:1] + got[1:2] * float(ROWS)
+    adding = ones_where((iota((CORES * ROWS, SLOTS), 0) + 1).astype(jnp.float32) == wanted)
+    adder[...] = adding.astype(bf16)
+    pick[...] = adding.T.astype(bf16)
+    late = jnp.sum(got[2:3], axis=1, keepdims=True)
+
+    def pick_rows(k):
+        own_in(table_hbm, table, 1, k).wait()
+        mate_in(table_hbm, table, 2, k).wait_recv()
+        rows = table[k].reshape(CORES * ROWS, width)
+        for h in range(2):
+            at = slice(h * half, (h + 1) * half)
+            p_send[k, :, :, at] = dot(pick[...], rows[:, at]).astype(bf16).reshape(CHIPS, PAIR, half)
+        p_start(p_send.at[k], e1_recv.at[k], e1_sem.at[0, k], e1_sem.at[1, k], e1_sem.at[2, k])
+
+    pick_rows(0)
+    flag_send[...] = jnp.broadcast_to(late, flag_send.shape)
+    z_start(flag_send, flag_recv, late_sem.at[0], late_sem.at[1], late_sem.at[2])
+
+    def first_hop(k):
+        pack_grads(k)
+        pick_rows(k)
+
+    loop(1, CHUNKS, first_hop)
+
+    def second_hop(k):
+        wait_recv(e1_recv.at[k], CHIPS, e1_sem.at[1, k], e1_sem.at[2, k])
+        wait_bytes(z_send.at[k], PLANES - 1, g1_sem.at[0, k])
+        wait_recv(g1_recv.at[k], PLANES, g1_sem.at[1, k], g1_sem.at[2, k])
+        store_z(k, unspread[...], e1_recv[k].reshape(SLOTS, width))
+        z_start(z_send.at[k], e2_recv.at[k], e2_sem.at[0, k], e2_sem.at[1, k], e2_sem.at[2, k])
+        wait_bytes(p_send.at[k], CHIPS - 1, e1_sem.at[0, k])
+        for h in range(2):
+            out = dot(spread[...], load_z(g1_recv, k, h)).astype(bf16)
+            p_send[k, :, :, h * half : (h + 1) * half] = out.reshape(CHIPS, PAIR, half)
+        p_start(p_send.at[k], g2_recv.at[k], g2_sem.at[0, k], g2_sem.at[1, k], g2_sem.at[2, k])
+
+    loop(0, CHUNKS, second_hop)
+
+    def own_out(vmem, hbm, i, k):
+        return pltpu.make_async_copy(vmem.at[k, core], hbm.at[:, columns(core, k)], out_sem.at[i, k])
+
+    def mate_out(vmem, hbm, i, k):
+        return pltpu.make_async_remote_copy(
+            src_ref=vmem.at[k, mate], dst_ref=hbm.at[:, columns(core, k)],
+            send_sem=mate_sem.at[i, k], recv_sem=mate_sem.at[i + 1, k],
+            device_id=device(z, p, mate), device_id_type=MESH,
+        )
+
+    def finish(k):
+        wait_recv(e2_recv.at[k], PLANES, e2_sem.at[1, k], e2_sem.at[2, k])
+        for h in range(2):
+            out = dot(unpack[...], load_z(e2_recv, k, h)).astype(bf16)
+            emb[k, :, :, h * half : (h + 1) * half] = out.reshape(CORES, TOKS, half)
+        mate_out(emb, emb_hbm, 4, k).start()
+        own_out(emb, emb_hbm, 0, k).start()
+        wait_recv(g2_recv.at[k], CHIPS, g2_sem.at[1, k], g2_sem.at[2, k])
+        rows = g2_recv[k].reshape(SLOTS, width)
+        for h in range(2):
+            out = dot(adder[...], rows[:, h * half : (h + 1) * half]).astype(bf16)
+            tgr[k, :, :, h * half : (h + 1) * half] = out.reshape(CORES, ROWS, half)
+        mate_out(tgr, tgr_hbm, 6, k).start()
+        own_out(tgr, tgr_hbm, 1, k).start()
+
+    loop(0, CHUNKS, finish)
+    wait_recv(flag_recv, PLANES, late_sem.at[1], late_sem.at[2])
+    flag_ref[0, 0] = jnp.max(flag_recv[...])
+
+    def drain(k):
+        mate_in(grads_hbm, grads, 0, k).wait_send()
+        mate_in(table_hbm, table, 2, k).wait_send()
+        wait_bytes(z_send.at[k], PLANES - 1, e2_sem.at[0, k])
+        wait_bytes(p_send.at[k], CHIPS - 1, g2_sem.at[0, k])
+        own_out(emb, emb_hbm, 0, k).wait()
+        own_out(tgr, tgr_hbm, 1, k).wait()
+        mate_out(emb, emb_hbm, 4, k).wait()
+        mate_out(tgr, tgr_hbm, 6, k).wait()
+
+    loop(0, CHUNKS, drain)
+    wait_bytes(zreq_send, PLANES - 1, req_sem.at[2])
+    wait_bytes(preq_send, CHIPS - 1, req_sem.at[5])
+    wait_bytes(flag_send, PLANES - 1, late_sem.at[0])
+
+
+def routed(embedding_table, token_ids, output_grads):
+    depth = embedding_table.shape[1]
+    width = depth // (CORES * CHUNKS)
+    bf16, f32 = jnp.bfloat16, jnp.float32
+    anywhere = pl.BlockSpec(memory_space=pl.ANY)
+    dma = pltpu.SemaphoreType.DMA
+    toks, rows = CORES * TOKS, CORES * ROWS
+    z_block = pltpu.VMEM((CHUNKS, PLANES, 2 * POOL, width // 2), bf16)
+    p_block = pltpu.VMEM((CHUNKS, CHIPS, PAIR, width), bf16)
+    row_block = pltpu.VMEM((CHUNKS, CORES, ROWS, width), bf16)
+    tok_block = pltpu.VMEM((CHUNKS, CORES, TOKS, width), bf16)
+    z_note = pltpu.VMEM((PLANES, 8, LANE), f32)
+    p_note = pltpu.VMEM((CHIPS, 8, CHIPS // 2 * PAIR), f32)
+    return pl.pallas_call(
+        kernel,
+        out_shape=(
+            jax.ShapeDtypeStruct((TOKS, depth), bf16),
+            jax.ShapeDtypeStruct((ROWS, depth), bf16),
+            jax.ShapeDtypeStruct((1, 1), f32),
+        ),
+        in_specs=[pl.BlockSpec(memory_space=pltpu.VMEM), anywhere, anywhere],
+        out_specs=(anywhere, anywhere, pl.BlockSpec(memory_space=pltpu.SMEM)),
+        scratch_shapes=[
+            row_block, tok_block, tok_block, row_block,
+            z_block, z_block, z_block,
+            p_block, p_block, p_block,
+            pltpu.VMEM((8, TOKS), jnp.int32), pltpu.VMEM((CORES, 8, TOKS), jnp.int32),
+            z_note, z_note, p_note, p_note, z_note, z_note,
+            pltpu.VMEM((ENTRIES, toks), bf16),
+            pltpu.VMEM((toks, ENTRIES), bf16),
+            pltpu.VMEM((SLOTS, ENTRIES), bf16),
+            pltpu.VMEM((ENTRIES, SLOTS), bf16),
+            pltpu.VMEM((SLOTS, rows), bf16),
+            pltpu.VMEM((rows, SLOTS), bf16),
+            dma((2, CHUNKS)),
+            dma((2, CHUNKS)),
+            dma((8, CHUNKS)),
+            dma((3,)),
+            dma((8,)),
+            dma((3, CHUNKS)),
+            dma((3, CHUNKS)),
+            dma((3, CHUNKS)),
+            dma((3, CHUNKS)),
+        ],
+        compiler_params=pltpu.CompilerParams(
+            collective_id=0, has_side_effects=True, vmem_limit_bytes=56 * 1024 * 1024
+        ),
+    )(token_ids.reshape(1, TOKS), embedding_table, output_grads)
+
+
+def on_device(embedding_table, token_ids, output_grads):
+    embedded, table_grads, late = routed(embedding_table, token_ids, output_grads)
+
+    def again(_):
+        emb, tgr = general(embedding_table, token_ids, output_grads)
+        return emb, tgr, jnp.float32(0)
+
+    embedded, table_grads, _ = lax.while_loop(
+        lambda held: held[2] > 0, again, (embedded, table_grads, late[0, 0])
+    )
+    return embedded, table_grads
 
 
 def solution(mesh):

time: 454 us -> 188 us (0.41)
  waiting for transfers between devices: 328 us -> 0 us
  Pallas kernels: 0 us -> 181 us
  local copies, waits for them, and re-layouts: 55.5 us -> 5.27 us
  starting transfers between devices: 39.3 us -> 0 us
  matrix products: 27 us -> 0 us
    all_to_all x3 -> x0, waiting for transfers between devices: 328 us -> none  [the longest x1 165 us: on_device(): lax.all_to_all(picked, 'vocab', split_axis=0, concat_axis=0, tiled=True)]
    pallas_call x0 -> x1, Pallas kernels: none -> 181 us  [routed(): pl.pallas_call(kernel, out_shape=(jax.ShapeDtypeStruct((TOKS, depth), bf1...]
    reshape x4 -> x0, local copies, waits for them, and re-layouts: 54.6 us -> none  [the longest x1 14.2 us: on_device(): picked = picked.astype(jnp.bfloat16).reshape(devices, capacity, width)]
    all_to_all x3 -> x0, starting transfers between devices: 39.3 us -> none  [the longest x1 15.7 us: on_device(): lax.all_to_all(request.reshape(devices, capacity), 'vocab', split_axis=0,...]
    dot_general x4 -> x0, matrix products: 27 us -> none  [the longest x1 7.78 us: on_device(): jnp.dot(picker, embedding_table, preferred_element_type=jnp.float32)]
    unnamed x4 -> x8, local copies, waits for them, and re-layouts: 0.02 us -> 5.27 us
  transfers between devices with their start and end apart: 3 -> 0, of which waited for: 2 -> 0; matrix products, arithmetic and copies ran while one was open for 14% -> 0% of each run, Pallas kernels for 0% -> 0%
where the time goes in v2:
time: 188 us
  Pallas kernels  181 us (96%)
  local copies, waits for them, and re-layouts  5.27 us (3%)
    pallas_call x1, Pallas kernels, routed(): pl.pallas_call(kernel, out_shape=(jax.ShapeDtypeStruct((TOKS, depth), bf1...  181 us
    unnamed x8, local copies, waits for them, and re-layouts  5.27 us

profile of v2, /device:TPU:1, one launch (start us, length us, event | category | flops | bytes accessed | tf_op | source)
XLA Modules:
  0.0 187.7 jit_solution(12053992096690768087)
XLA Ops:
  0.6 0.0 copy-start.2
  0.6 0.0 copy-start
  0.6 181.0 %shard_map.50 = (bf16[128,8192]{1,0:T(8,128)(2,1)}, bf16[256,8192]{1,0:T(8,128)(2,1)}, f32[1,1]{1,0:T(1,128)}) custom-call(s32[1,128]{1,0:T(1,128)} %bitcast.7, bf16[256,8192]{1,0:T(8,128)(2,1)} %table_hbm.1, bf16[128,8192]{1,0:T(8,128)(2,1)} %grads_hbm.1), custom_call_target="tpu_custom_call" | custom-call | tf_op jit(solution)/shard_map/pallas_call | solution.py:369
  181.7 0.0 copy-done.2
  181.7 0.0 copy-done
  181.7 0.8 while.11
  182.5 0.0 copy-start.1
  182.5 3.2 %copy.20 = bf16[128,8192]{1,0:T(8,128)(2,1)} copy(bf16[128,8192]{1,0:T(8,128)(2,1)} %get-tuple-element.80) | data formatting | bytes 4194304
  185.7 0.0 copy-done.1
  185.7 2.0 %copy.21 = bf16[256,8192]{1,0:T(8,128)(2,1)} copy(bf16[256,8192]{1,0:T(8,128)(2,1)S(1)} %copy-done.1) | data formatting | bytes 8388608
Async XLA Ops:
  0.6 181.0 %copy-start.2 = (s32[128]{0:T(128)S(1)}, s32[128]{0:T(128)}, u32[]{:S(2)}) copy-start(s32[128]{0:T(128)} %param.6) | copy-start | bytes 1540
  0.6 181.0 %copy-start = (bf16[128,8192]{1,0:T(8,128)(2,1)S(1)}, bf16[128,8192]{1,0:T(8,128)(2,1)}, u32[]{:S(2)}) copy-start(bf16[128,8192]{1,0:T(8,128)(2,1)} %grads_hbm.1) | copy-start | bytes 6291460
  182.5 3.3 %copy-start.1 = (bf16[256,8192]{1,0:T(8,128)(2,1)S(1)}, bf16[256,8192]{1,0:T(8,128)(2,1)}, u32[]{:S(2)}) copy-start(bf16[256,8192]{1,0:T(8,128)(2,1)} %get-tuple-element.81) | copy-start | bytes 12582916

commit v3 on v2

--- a/solution.py
+++ b/solution.py
@@ -12,12 +12,16 @@
 ROWS = 256
 TOKS = 128
 LANE = 128
-POOL = 56
-STRIDE = 64
+BLOCK = 16
+POOL = 48
+PASS = 16
 PAIR = 48
-CHUNKS = 4
-ENTRIES = PLANES * STRIDE
+CHUNKS = 8
+LEAD = 3
+FIRST = PLANES * POOL
 SLOTS = CHIPS * PAIR
+SPARE = LANE
+ENTRIES = FIRST + SPARE
 
 
 def ranks_within(owners):
@@ -95,10 +99,12 @@
     table, grads, emb, tgr,
     z_send, g1_recv, e2_recv,
     p_send, e1_recv, g2_recv,
+    on_send, back_send,
     ids_send, ids_recv, zreq_send, zreq_recv, preq_send, preq_recv, flag_send, flag_recv,
-    pack, unpack, spread, unspread, pick, adder,
-    in_sem, out_sem, mate_sem, late_sem, req_sem,
-    g1_sem, e1_sem, g2_sem, e2_sem,
+    onreq_send, onreq_recv,
+    pack, unpack, spread, unspread, pick, adder, take, give,
+    in_sem, out_sem, mate_sem, late_sem, req_sem, onreq_sem,
+    g1_sem, e1_sem, g2_sem, e2_sem, on_sem, back_sem,
 ):
     me = lax.axis_index("vocab")
     core = lax.rem(me, CORES)
@@ -108,6 +114,7 @@
     width = table.shape[3]
     half = width // 2
     bf16 = jnp.bfloat16
+    z_blocks, p_blocks = FIRST // BLOCK, SLOTS // BLOCK
 
     def device(plane, chip, which):
         return ((plane * CHIPS + chip) * CORES + which,)
@@ -141,6 +148,15 @@
     loop(0, CHUNKS, lambda k: own_in(grads_hbm, grads, 0, k).start())
     loop(0, CHUNKS, lambda k: own_in(table_hbm, table, 1, k).start())
 
+    def clear(k):
+        first = z_blocks + 2
+        count = SPARE // BLOCK - 2
+        g1_recv[k, pl.ds(first, count)] = jnp.zeros((count, BLOCK, width), bf16)
+        first = p_blocks + 2
+        e1_recv[k, pl.ds(first, count)] = jnp.zeros((count, BLOCK, width), bf16)
+
+    loop(0, CHUNKS, clear)
+
     barrier = pltpu.get_barrier_semaphore()
 
     def greet(plane, chip, which):
@@ -150,34 +166,48 @@
     loop(1, PLANES, lambda j: greet(z_peer(j), p, core))
     loop(1, CHIPS, lambda j: greet(z, p_peer(j), core))
 
-    def z_start(src, dst, send, recv, own):
+    def z_start(src, dst, send, recv, own, count=1):
+        def at(ref, t):
+            return ref.at[pl.ds(t * count, count)]
+
         def one(j):
             t = z_peer(j)
             pltpu.make_async_remote_copy(
-                src_ref=src.at[t], dst_ref=dst.at[z], send_sem=send, recv_sem=recv,
+                src_ref=at(src, t), dst_ref=at(dst, z), send_sem=send, recv_sem=recv,
                 device_id=device(t, p, core), device_id_type=MESH,
             ).start()
 
         loop(1, PLANES, one)
-        pltpu.make_async_copy(src.at[z], dst.at[z], own).start()
-
-    def p_start(src, dst, send, recv, own):
+        pltpu.make_async_copy(at(src, z), at(dst, z), own).start()
+
+    def p_start(src, dst, send, recv, own, count=1):
+        def at(ref, t):
+            return ref.at[pl.ds(t * count, count)]
+
         def one(j):
             t = p_peer(j)
             pltpu.make_async_remote_copy(
-                src_ref=src.at[t], dst_ref=dst.at[p], send_sem=send, recv_sem=recv,
+                src_ref=at(src, t), dst_ref=at(dst, p), send_sem=send, recv_sem=recv,
                 device_id=device(z, t, core), device_id_type=MESH,
             ).start()
 
         loop(1, CHIPS, one)
-        pltpu.make_async_copy(src.at[p], dst.at[p], own).start()
+        pltpu.make_async_copy(at(src, p), at(dst, p), own).start()
+
+    def passed(src, dst, sem, first, side):
+        t = lax.rem(z + (1 if side == 0 else PLANES - 1), PLANES)
+        return pltpu.make_async_remote_copy(
+            src_ref=src.at[side], dst_ref=dst.at[first + side],
+            send_sem=sem(side), recv_sem=sem(2 + side),
+            device_id=device(t, p, core), device_id_type=MESH,
+        )
 
     def wait_bytes(ref, count, sem):
         pltpu.make_async_copy(ref.at[pl.ds(0, count)], ref.at[pl.ds(0, count)], sem).wait()
 
-    def wait_recv(dst, count, recv, own):
-        wait_bytes(dst, count - 1, recv)
-        wait_bytes(dst, 1, own)
+    def wait_recv(dst, peers, recv, own, count=1):
+        wait_bytes(dst, (peers - 1) * count, recv)
+        wait_bytes(dst, count, own)
 
     ids_send[...] = jnp.broadcast_to(ids_ref[...], ids_send.shape)
     ids_recv[core] = ids_send[...]
@@ -203,53 +233,72 @@
     plane = lax.shift_right_logical(ids, 13)
     owner = lax.shift_right_logical(ids, 8)
     place = ranks(plane, PLANES, toks)
+    over = place >= POOL
+    ahead = (plane - z + PLANES) & (PLANES - 1)
+    up = (ahead >= 1) & (ahead <= PLANES // 2)
+    mark = jnp.where(over, jnp.where(up, 1, 2), 0)
+    there = (plane + jnp.where(over, jnp.where(up, PLANES - 1, 1), 0)) & (PLANES - 1)
+    same = ones_where(iota((PLANES, toks), 0) == plane)
+    held = jnp.minimum(jnp.sum(same, axis=1, keepdims=True), float(POOL))
+    here = ones_where(iota((PLANES, toks), 0) == there)
+    held = jnp.sum(here * held, axis=0, keepdims=True).astype(jnp.int32)
+    place = jnp.where(over, held + ranks(jnp.where(over, there, -1), PLANES, toks), place)
+    plane = there
     late = ones_where(jnp.max(place, axis=1, keepdims=True) >= POOL)
     fits = place < POOL
-    packer = ones_where(iota((ENTRIES, toks), 0) == jnp.where(fits, plane * STRIDE + place, -1))
+    packer = ones_where(iota((FIRST, toks), 0) == jnp.where(fits, plane * POOL + place, -1))
     pack[...] = packer.astype(bf16)
     row_code = ((ids & (ROWS - 1)) + 1).astype(jnp.float32)
     owner_code = (owner & (CHIPS * CORES - 1)).astype(jnp.float32)
     line = iota((PLANES * 8, toks), 0)
     part = line & 7
     fields = jnp.where(part == 0, row_code, jnp.where(part == 1, owner_code, 0.0))
+    fields = jnp.where(part == 3, mark.astype(jnp.float32), fields)
     fields = jnp.where((line >> 3) == plane, fields, 0.0)
-    lane_at = jnp.where(fits, lax.rem(z, 2) * STRIDE + place, -1)
-    where_at = ones_where(iota((LANE, toks), 0) == lane_at)
-    message = dot_nt(fields, where_at) + jnp.where(iota((PLANES * 8, LANE), 0) & 7 == 2, late, 0.0)
-    zreq_send[...] = message.reshape(PLANES, 8, LANE)
+    where_at = ones_where(iota((FIRST, toks), 0) == jnp.where(fits, z * POOL + place, -1))
+    message = dot_nt(fields, where_at) + jnp.where(iota((PLANES * 8, FIRST), 0) & 7 == 2, late, 0.0)
+    zreq_send[...] = message.reshape(PLANES, 8, FIRST)
     z_start(zreq_send, zreq_recv, req_sem.at[2], req_sem.at[3], req_sem.at[4])
 
-    def store_z(k, matrix, rows):
-        parts = []
+    def store(ref, k, matrix, rows):
         for h in range(2):
-            out = dot(matrix, rows[:, h * half : (h + 1) * half])
-            parts.append(out.reshape(PLANES, STRIDE, half)[:, :POOL])
-        z_send[k] = jnp.concatenate(parts, axis=1).astype(bf16)
-
-    def load_z(ref, k, h):
-        rows = ref[k].astype(jnp.float32)[:, h * POOL : (h + 1) * POOL]
-        rows = jnp.concatenate([rows, jnp.zeros((PLANES, STRIDE - POOL, half), jnp.float32)], axis=1)
-        return rows.reshape(ENTRIES, half).astype(bf16)
+            cols = slice(h * half, (h + 1) * half)
+            out = dot(matrix, rows[:, cols]).astype(bf16)
+            ref[k, :, :, cols] = out.reshape(ref.shape[1], BLOCK, half)
 
     def pack_grads(k):
         own_in(grads_hbm, grads, 0, k).wait()
         mate_in(grads_hbm, grads, 0, k).wait_recv()
-        store_z(k, pack[...], grads[k].reshape(toks, width))
-        z_start(z_send.at[k], g1_recv.at[k], g1_sem.at[0, k], g1_sem.at[1, k], g1_sem.at[2, k])
-
-    pack_grads(0)
-    unpack[...] = packer.T.astype(bf16)
+        store(z_send, k, pack[...], grads[k].reshape(toks, width))
+        z_start(z_send.at[k], g1_recv.at[k], g1_sem.at[0, k], g1_sem.at[1, k], g1_sem.at[2, k], POOL // BLOCK)
+
 
     wait_recv(zreq_recv, PLANES, req_sem.at[3], req_sem.at[4])
     got = zreq_recv[...]
-    got = jnp.concatenate([got[2 * g] + got[2 * g + 1] for g in range(PLANES // 2)], axis=1)
+    got = got.sum(axis=0)
+    late = jnp.sum(got[2:3], axis=1, keepdims=True)
+    mark = got[3:4].astype(jnp.int32)
+    turn = ranks(mark - 1, 2, FIRST)
+    late = late + ones_where(jnp.max(jnp.where(mark > 0, turn, 0), axis=1, keepdims=True) >= PASS)
+    pass_at = jnp.where((mark > 0) & (turn < PASS), (mark - 1) * PASS + turn, -1)
+    taker = ones_where(iota((SPARE, FIRST), 0) == pass_at)
+    take[...] = taker[: 2 * PASS].astype(bf16)
+    message = dot_nt(jnp.concatenate([got[0:2], jnp.zeros((6, FIRST), jnp.float32)], axis=0), taker)
+    lane = iota((8, LANE), 1)
+    onreq_send[0] = jnp.where(lane < PASS, message, 0.0)
+    onreq_send[1] = jnp.where(lane >= PASS, message, 0.0)
+    for side in range(2):
+        passed(onreq_send, onreq_recv, lambda i: onreq_sem.at[i], 0, side).start()
+    got = jnp.where(mark > 0, 0.0, got)
+    for side in range(2):
+        passed(onreq_send, onreq_recv, lambda i: onreq_sem.at[i], 0, side).wait()
+    got = jnp.concatenate([got, onreq_recv[0] + onreq_recv[1]], axis=1)
     entry_row = got[0:1]
     entry_owner = got[1:2].astype(jnp.int32)
     valid = entry_row > 0.0
     entry_chip = jnp.where(valid, entry_owner >> 1, -1)
     entry_core = (entry_owner & 1).astype(jnp.float32)
     place = ranks(entry_chip, CHIPS, ENTRIES)
-    late = jnp.sum(got[2:3], axis=1, keepdims=True)
     late = late + ones_where(jnp.max(place, axis=1, keepdims=True) >= PAIR)
     fits = valid & (place < PAIR)
     line = iota((CHIPS * 8, ENTRIES), 0)
@@ -262,9 +311,13 @@
     message = dot_nt(fields, where_at) + jnp.where(iota((CHIPS * 8, lanes), 0) & 7 == 2, late, 0.0)
     preq_send[...] = message.reshape(CHIPS, 8, lanes)
     p_start(preq_send, preq_recv, req_sem.at[5], req_sem.at[6], req_sem.at[7])
+    pack_grads(0)
+    unpack[...] = packer.T.astype(bf16)
     spreader = ones_where(iota((SLOTS, ENTRIES), 0) == jnp.where(fits, entry_chip * PAIR + place, -1))
     spread[...] = spreader.astype(bf16)
-    unspread[...] = spreader.T.astype(bf16)
+    returned = [taker[PASS : 2 * PASS], taker[:PASS], taker[2 * PASS :]]
+    unspread[...] = jnp.concatenate([spreader[:, :FIRST]] + returned, axis=0).T.astype(bf16)
+    give[...] = spreader[:, FIRST:].T[: 2 * PASS].astype(bf16)
 
     wait_recv(preq_recv, CHIPS, req_sem.at[6], req_sem.at[7])
     got = preq_recv[...]
@@ -278,11 +331,8 @@
     def pick_rows(k):
         own_in(table_hbm, table, 1, k).wait()
         mate_in(table_hbm, table, 2, k).wait_recv()
-        rows = table[k].reshape(CORES * ROWS, width)
-        for h in range(2):
-            at = slice(h * half, (h + 1) * half)
-            p_send[k, :, :, at] = dot(pick[...], rows[:, at]).astype(bf16).reshape(CHIPS, PAIR, half)
-        p_start(p_send.at[k], e1_recv.at[k], e1_sem.at[0, k], e1_sem.at[1, k], e1_sem.at[2, k])
+        store(p_send, k, pick[...], table[k].reshape(CORES * ROWS, width))
+        p_start(p_send.at[k], e1_recv.at[k], e1_sem.at[0, k], e1_sem.at[1, k], e1_sem.at[2, k], PAIR // BLOCK)
 
     pick_rows(0)
     flag_send[...] = jnp.broadcast_to(late, flag_send.shape)
@@ -292,21 +342,53 @@
         pack_grads(k)
         pick_rows(k)
 
-    loop(1, CHUNKS, first_hop)
+    loop(1, LEAD, first_hop)
+
+    def on(k, side):
+        return passed(on_send.at[k], g1_recv.at[k], lambda i: on_sem.at[i, k], z_blocks, side)
+
+    def back(k, side):
+        return passed(back_send.at[k], e1_recv.at[k], lambda i: back_sem.at[i, k], p_blocks, side)
+
+    def pass_on(k):
+        wait_recv(g1_recv.at[k], PLANES, g1_sem.at[1, k], g1_sem.at[2, k], POOL // BLOCK)
+        rows = g1_recv[k, pl.ds(0, z_blocks)].reshape(FIRST, width)
+        on_send[k] = dot(take[...], rows).astype(bf16).reshape(2, PASS, width)
+        for side in range(2):
+            on(k, side).start()
+        wait_recv(e1_recv.at[k], CHIPS, e1_sem.at[1, k], e1_sem.at[2, k], PAIR // BLOCK)
+        rows = e1_recv[k, pl.ds(0, p_blocks)].reshape(SLOTS, width)
+        rows = dot(give[...], rows).astype(bf16).reshape(2, PASS, width)
+        back_send[k, 0] = rows[1]
+        back_send[k, 1] = rows[0]
+        for side in range(2):
+            back(k, side).start()
 
     def second_hop(k):
-        wait_recv(e1_recv.at[k], CHIPS, e1_sem.at[1, k], e1_sem.at[2, k])
-        wait_bytes(z_send.at[k], PLANES - 1, g1_sem.at[0, k])
-        wait_recv(g1_recv.at[k], PLANES, g1_sem.at[1, k], g1_sem.at[2, k])
-        store_z(k, unspread[...], e1_recv[k].reshape(SLOTS, width))
-        z_start(z_send.at[k], e2_recv.at[k], e2_sem.at[0, k], e2_sem.at[1, k], e2_sem.at[2, k])
-        wait_bytes(p_send.at[k], CHIPS - 1, e1_sem.at[0, k])
-        for h in range(2):
-            out = dot(spread[...], load_z(g1_recv, k, h)).astype(bf16)
-            p_send[k, :, :, h * half : (h + 1) * half] = out.reshape(CHIPS, PAIR, half)
-        p_start(p_send.at[k], g2_recv.at[k], g2_sem.at[0, k], g2_sem.at[1, k], g2_sem.at[2, k])
-
-    loop(0, CHUNKS, second_hop)
+        wait_bytes(z_send.at[k], (PLANES - 1) * (POOL // BLOCK), g1_sem.at[0, k])
+        for side in range(2):
+            back(k, side).wait_recv()
+        store(z_send, k, unspread[...], e1_recv[k].reshape(SLOTS + SPARE, width))
+        z_start(z_send.at[k], e2_recv.at[k], e2_sem.at[0, k], e2_sem.at[1, k], e2_sem.at[2, k], POOL // BLOCK)
+        wait_bytes(p_send.at[k], (CHIPS - 1) * (PAIR // BLOCK), e1_sem.at[0, k])
+        for side in range(2):
+            on(k, side).wait_recv()
+        store(p_send, k, spread[...], g1_recv[k].reshape(ENTRIES, width))
+        p_start(p_send.at[k], g2_recv.at[k], g2_sem.at[0, k], g2_sem.at[1, k], g2_sem.at[2, k], PAIR // BLOCK)
+
+    def turn_round(k):
+        pass_on(k)
+        second_hop(k - 1)
+
+    def whole_step(k):
+        turn_round(k)
+        first_hop(k + LEAD)
+
+    pass_on(0)
+    first_hop(LEAD)
+    loop(1, CHUNKS - LEAD, whole_step)
+    loop(CHUNKS - LEAD, CHUNKS, turn_round)
+    second_hop(CHUNKS - 1)
 
     def own_out(vmem, hbm, i, k):
         return pltpu.make_async_copy(vmem.at[k, core], hbm.at[:, columns(core, k)], out_sem.at[i, k])
@@ -319,17 +401,18 @@
         )
 
     def finish(k):
-        wait_recv(e2_recv.at[k], PLANES, e2_sem.at[1, k], e2_sem.at[2, k])
+        wait_recv(e2_recv.at[k], PLANES, e2_sem.at[1, k], e2_sem.at[2, k], POOL // BLOCK)
+        rows = e2_recv[k].reshape(FIRST, width)
         for h in range(2):
-            out = dot(unpack[...], load_z(e2_recv, k, h)).astype(bf16)
-            emb[k, :, :, h * half : (h + 1) * half] = out.reshape(CORES, TOKS, half)
+            cols = slice(h * half, (h + 1) * half)
+            emb[k, :, :, cols] = dot(unpack[...], rows[:, cols]).astype(bf16).reshape(CORES, TOKS, half)
         mate_out(emb, emb_hbm, 4, k).start()
         own_out(emb, emb_hbm, 0, k).start()
-        wait_recv(g2_recv.at[k], CHIPS, g2_sem.at[1, k], g2_sem.at[2, k])
+        wait_recv(g2_recv.at[k], CHIPS, g2_sem.at[1, k], g2_sem.at[2, k], PAIR // BLOCK)
         rows = g2_recv[k].reshape(SLOTS, width)
         for h in range(2):
-            out = dot(adder[...], rows[:, h * half : (h + 1) * half]).astype(bf16)
-            tgr[k, :, :, h * half : (h + 1) * half] = out.reshape(CORES, ROWS, half)
+            cols = slice(h * half, (h + 1) * half)
+            tgr[k, :, :, cols] = dot(adder[...], rows[:, cols]).astype(bf16).reshape(CORES, ROWS, half)
         mate_out(tgr, tgr_hbm, 6, k).start()
         own_out(tgr, tgr_hbm, 1, k).start()
 
@@ -340,8 +423,11 @@
     def drain(k):
         mate_in(grads_hbm, grads, 0, k).wait_send()
         mate_in(table_hbm, table, 2, k).wait_send()
-        wait_bytes(z_send.at[k], PLANES - 1, e2_sem.at[0, k])
-        wait_bytes(p_send.at[k], CHIPS - 1, g2_sem.at[0, k])
+        wait_bytes(z_send.at[k], (PLANES - 1) * (POOL // BLOCK), e2_sem.at[0, k])
+        wait_bytes(p_send.at[k], (CHIPS - 1) * (PAIR // BLOCK), g2_sem.at[0, k])
+        for side in range(2):
+            on(k, side).wait_send()
+            back(k, side).wait_send()
         own_out(emb, emb_hbm, 0, k).wait()
         own_out(tgr, tgr_hbm, 1, k).wait()
         mate_out(emb, emb_hbm, 4, k).wait()
@@ -360,11 +446,15 @@
     anywhere = pl.BlockSpec(memory_space=pl.ANY)
     dma = pltpu.SemaphoreType.DMA
     toks, rows = CORES * TOKS, CORES * ROWS
-    z_block = pltpu.VMEM((CHUNKS, PLANES, 2 * POOL, width // 2), bf16)
-    p_block = pltpu.VMEM((CHUNKS, CHIPS, PAIR, width), bf16)
+
+    def blocks(count):
+        return pltpu.VMEM((CHUNKS, count // BLOCK, BLOCK, width), bf16)
+
     row_block = pltpu.VMEM((CHUNKS, CORES, ROWS, width), bf16)
     tok_block = pltpu.VMEM((CHUNKS, CORES, TOKS, width), bf16)
-    z_note = pltpu.VMEM((PLANES, 8, LANE), f32)
+    z_note = pltpu.VMEM((PLANES, 8, FIRST), f32)
+    late_note = pltpu.VMEM((PLANES, 8, LANE), f32)
+    on_note = pltpu.VMEM((2, 8, LANE), f32)
     p_note = pltpu.VMEM((CHIPS, 8, CHIPS // 2 * PAIR), f32)
     return pl.pallas_call(
         kernel,
@@ -377,25 +467,32 @@
         out_specs=(anywhere, anywhere, pl.BlockSpec(memory_space=pltpu.SMEM)),
         scratch_shapes=[
             row_block, tok_block, tok_block, row_block,
-            z_block, z_block, z_block,
-            p_block, p_block, p_block,
+            blocks(FIRST), blocks(ENTRIES), blocks(FIRST),
+            blocks(SLOTS), blocks(SLOTS + SPARE), blocks(SLOTS),
+            blocks(2 * PASS), blocks(2 * PASS),
             pltpu.VMEM((8, TOKS), jnp.int32), pltpu.VMEM((CORES, 8, TOKS), jnp.int32),
-            z_note, z_note, p_note, p_note, z_note, z_note,
-            pltpu.VMEM((ENTRIES, toks), bf16),
-            pltpu.VMEM((toks, ENTRIES), bf16),
+            z_note, z_note, p_note, p_note, late_note, late_note,
+            on_note, on_note,
+            pltpu.VMEM((FIRST, toks), bf16),
+            pltpu.VMEM((toks, FIRST), bf16),
             pltpu.VMEM((SLOTS, ENTRIES), bf16),
-            pltpu.VMEM((ENTRIES, SLOTS), bf16),
+            pltpu.VMEM((FIRST, SLOTS + SPARE), bf16),
             pltpu.VMEM((SLOTS, rows), bf16),
             pltpu.VMEM((rows, SLOTS), bf16),
+            pltpu.VMEM((2 * PASS, FIRST), bf16),
+            pltpu.VMEM((2 * PASS, SLOTS), bf16),
             dma((2, CHUNKS)),
             dma((2, CHUNKS)),
             dma((8, CHUNKS)),
             dma((3,)),
             dma((8,)),
+            dma((4,)),
             dma((3, CHUNKS)),
             dma((3, CHUNKS)),
             dma((3, CHUNKS)),
             dma((3, CHUNKS)),
+            dma((4, CHUNKS)),
+            dma((4, CHUNKS)),
         ],
         compiler_params=pltpu.CompilerParams(
             collective_id=0, has_side_effects=True, vmem_limit_bytes=56 * 1024 * 1024

time: 188 us -> 177 us (0.941)
  Pallas kernels: 181 us -> 171 us
    pallas_call x1, Pallas kernels: 181 us -> 171 us  [routed(): pl.pallas_call(kernel, out_shape=(jax.ShapeDtypeStruct((TOKS, depth), bf1...]
where the time goes in v3:
time: 177 us
  Pallas kernels  171 us (97%)
  local copies, waits for them, and re-layouts  5.27 us (3%)
    pallas_call x1, Pallas kernels, routed(): pl.pallas_call(kernel, out_shape=(jax.ShapeDtypeStruct((TOKS, depth), bf1...  171 us
    unnamed x8, local copies, waits for them, and re-layouts  5.27 us

profile of v3, /device:TPU:1, one launch (start us, length us, event | category | flops | bytes accessed | tf_op | source)
XLA Modules:
  0.0 177.3 jit_solution(9290830481231035392)
XLA Ops:
  0.6 0.0 copy-start.2
  0.6 0.0 copy-start
  0.6 170.5 %shard_map.50 = (bf16[128,8192]{1,0:T(8,128)(2,1)}, bf16[256,8192]{1,0:T(8,128)(2,1)}, f32[1,1]{1,0:T(1,128)}) custom-call(s32[1,128]{1,0:T(1,128)} %bitcast.7, bf16[256,8192]{1,0:T(8,128)(2,1)} %table_hbm.1, bf16[128,8192]{1,0:T(8,128)(2,1)} %grads_hbm.1), custom_call_target="tpu_custom_call" | custom-call | tf_op jit(solution)/shard_map/pallas_call | solution.py:459
  171.2 0.0 copy-done.2
  171.2 0.0 copy-done
  171.2 0.8 while.11
  172.0 0.0 copy-start.1
  172.0 3.2 %copy.20 = bf16[128,8192]{1,0:T(8,128)(2,1)} copy(bf16[128,8192]{1,0:T(8,128)(2,1)} %get-tuple-element.80) | data formatting | bytes 4194304
  175.3 0.0 copy-done.1
  175.3 2.0 %copy.21 = bf16[256,8192]{1,0:T(8,128)(2,1)} copy(bf16[256,8192]{1,0:T(8,128)(2,1)S(1)} %copy-done.1) | data formatting | bytes 8388608
Async XLA Ops:
  0.6 170.6 %copy-start.2 = (s32[128]{0:T(128)S(1)}, s32[128]{0:T(128)}, u32[]{:S(2)}) copy-start(s32[128]{0:T(128)} %param.6) | copy-start | bytes 1540
  0.6 170.6 %copy-start = (bf16[128,8192]{1,0:T(8,128)(2,1)S(1)}, bf16[128,8192]{1,0:T(8,128)(2,1)}, u32[]{:S(2)}) copy-start(bf16[128,8192]{1,0:T(8,128)(2,1)} %grads_hbm.1) | copy-start | bytes 6291460
  172.0 3.3 %copy-start.1 = (bf16[256,8192]{1,0:T(8,128)(2,1)S(1)}, bf16[256,8192]{1,0:T(8,128)(2,1)}, u32[]{:S(2)}) copy-start(bf16[256,8192]{1,0:T(8,128)(2,1)} %get-tuple-element.81) | copy-start | bytes 12582916

commit v4 on v3

--- a/solution.py
+++ b/solution.py
@@ -100,10 +100,9 @@
     z_send, g1_recv, e2_recv,
     p_send, e1_recv, g2_recv,
     on_send, back_send,
-    ids_send, ids_recv, zreq_send, zreq_recv, preq_send, preq_recv, flag_send, flag_recv,
-    onreq_send, onreq_recv,
+    ids_send, line_recv, preq_send, preq_recv, flag_send, flag_recv,
     pack, unpack, spread, unspread, pick, adder, take, give,
-    in_sem, out_sem, mate_sem, late_sem, req_sem, onreq_sem,
+    in_sem, out_sem, mate_sem, late_sem, req_sem,
     g1_sem, e1_sem, g2_sem, e2_sem, on_sem, back_sem,
 ):
     me = lax.axis_index("vocab")
@@ -162,8 +161,13 @@
     def greet(plane, chip, which):
         pl.semaphore_signal(barrier, inc=1, device_id=device(plane, chip, which), device_id_type=MESH)
 
-    greet(z, p, mate)
-    loop(1, PLANES, lambda j: greet(z_peer(j), p, core))
+    line_count = PLANES * CORES
+    line_me = z * CORES + core
+
+    def line_peer(j):
+        return lax.rem(line_me + j, line_count)
+
+    loop(1, line_count, lambda j: greet(line_peer(j) // CORES, p, lax.rem(line_peer(j), CORES)))
     loop(1, CHIPS, lambda j: greet(z, p_peer(j), core))
 
     def z_start(src, dst, send, recv, own, count=1):
@@ -210,19 +214,24 @@
         wait_bytes(dst, count, own)
 
     ids_send[...] = jnp.broadcast_to(ids_ref[...], ids_send.shape)
-    ids_recv[core] = ids_send[...]
-    pl.semaphore_wait(barrier, 1 + PLANES - 1 + CHIPS - 1)
-    ids_copy = pltpu.make_async_remote_copy(
-        src_ref=ids_send, dst_ref=ids_recv.at[core], send_sem=req_sem.at[0], recv_sem=req_sem.at[1],
-        device_id=device(z, p, mate), device_id_type=MESH,
-    )
-    ids_copy.start()
+    line_recv[line_me] = ids_send[...]
+    pl.semaphore_wait(barrier, line_count - 1 + CHIPS - 1)
+
+    def ids_copy(j):
+        t = line_peer(j)
+        return pltpu.make_async_remote_copy(
+            src_ref=ids_send, dst_ref=line_recv.at[line_me],
+            send_sem=req_sem.at[0], recv_sem=req_sem.at[1],
+            device_id=device(t // CORES, p, lax.rem(t, CORES)), device_id_type=MESH,
+        )
+
+    loop(1, line_count, lambda j: ids_copy(j).start())
     loop(0, CHUNKS, lambda k: mate_in(grads_hbm, grads, 0, k).start())
     loop(0, CHUNKS, lambda k: mate_in(table_hbm, table, 2, k).start())
-    ids_copy.wait()
-    got = ids_recv[...]
-    ids = jnp.concatenate([got[0, 0:1], got[1, 0:1]], axis=1)
+    wait_bytes(line_recv, line_count - 1, req_sem.at[1])
     toks = CORES * TOKS
+    got = line_recv[...].reshape(PLANES, CORES, 8, TOKS)
+    ids = jnp.concatenate([got[:, c].reshape(PLANES * 8, TOKS) for c in range(CORES)], axis=1)
 
     def ranks(keys, kinds, count):
         same = ones_where(iota((kinds, count), 0) == keys)
@@ -230,35 +239,86 @@
         before = dot(same.astype(bf16), earlier.astype(bf16))
         return jnp.sum(same * before, axis=0, keepdims=True).astype(jnp.int32)
 
+    shape = (PLANES * 8, toks)
+    chip = iota(shape, 0) >> 3
+    part = iota(shape, 0) & 7
+    earlier = ones_where(iota((toks, toks), 0) < iota((toks, toks), 1)).astype(bf16)
+
+    def before(mask):
+        return dot(mask.astype(bf16), earlier)
+
+    def over_parts(x):
+        x = jnp.sum(x.reshape(PLANES, 8, toks), axis=1, keepdims=True)
+        return jnp.broadcast_to(x, (PLANES, 8, toks)).reshape(shape).astype(jnp.int32)
+
     plane = lax.shift_right_logical(ids, 13)
     owner = lax.shift_right_logical(ids, 8)
-    place = ranks(plane, PLANES, toks)
+    same = ones_where(plane == part)
+    place = over_parts(same * before(same))
     over = place >= POOL
-    ahead = (plane - z + PLANES) & (PLANES - 1)
+    ahead = (plane - chip + PLANES) & (PLANES - 1)
     up = (ahead >= 1) & (ahead <= PLANES // 2)
     mark = jnp.where(over, jnp.where(up, 1, 2), 0)
     there = (plane + jnp.where(over, jnp.where(up, PLANES - 1, 1), 0)) & (PLANES - 1)
-    same = ones_where(iota((PLANES, toks), 0) == plane)
     held = jnp.minimum(jnp.sum(same, axis=1, keepdims=True), float(POOL))
-    here = ones_where(iota((PLANES, toks), 0) == there)
-    held = jnp.sum(here * held, axis=0, keepdims=True).astype(jnp.int32)
-    place = jnp.where(over, held + ranks(jnp.where(over, there, -1), PLANES, toks), place)
-    plane = there
-    late = ones_where(jnp.max(place, axis=1, keepdims=True) >= POOL)
+    here = ones_where(there == part)
+    moved = jnp.where(over, here, 0.0)
+    place = jnp.where(over, over_parts(here * held + moved * before(moved)), place)
     fits = place < POOL
-    packer = ones_where(iota((FIRST, toks), 0) == jnp.where(fits, plane * POOL + place, -1))
-    pack[...] = packer.astype(bf16)
+
+    def turns(to_next, to_last):
+        sent = jnp.where(part == 0, ones_where(there == to_next), ones_where(there == to_last))
+        sent = jnp.where(mark == part + 1, jnp.where(fits, sent, 0.0), 0.0)
+        count = jnp.broadcast_to(jnp.sum(sent, axis=1, keepdims=True), (PLANES * 8, LANE))
+        row, col = iota((PLANES * 8, PLANES * 8), 0), iota((PLANES * 8, PLANES * 8), 1)
+        sooner = ones_where(((col >> 3) < (row >> 3)) & ((col & 7) == (row & 7)))
+        sooner = dot(sooner.astype(bf16), count.astype(bf16))[:, :1]
+        return over_parts(sent) > 0, over_parts(sent * (before(sent) + sooner))
+
+    passing, turn = turns(z, z)
+    guest, seat = turns(z_peer(PLANES - 1), z_peer(1))
+    late = ones_where(jnp.logical_not(fits)) + ones_where(passing & (turn >= PASS))
+    late = jnp.max(jnp.max(late, axis=1, keepdims=True), axis=0, keepdims=True)
+
     row_code = ((ids & (ROWS - 1)) + 1).astype(jnp.float32)
     owner_code = (owner & (CHIPS * CORES - 1)).astype(jnp.float32)
-    line = iota((PLANES * 8, toks), 0)
-    part = line & 7
     fields = jnp.where(part == 0, row_code, jnp.where(part == 1, owner_code, 0.0))
-    fields = jnp.where(part == 3, mark.astype(jnp.float32), fields)
-    fields = jnp.where((line >> 3) == plane, fields, 0.0)
-    where_at = ones_where(iota((FIRST, toks), 0) == jnp.where(fits, z * POOL + place, -1))
-    message = dot_nt(fields, where_at) + jnp.where(iota((PLANES * 8, FIRST), 0) & 7 == 2, late, 0.0)
-    zreq_send[...] = message.reshape(PLANES, 8, FIRST)
-    z_start(zreq_send, zreq_recv, req_sem.at[2], req_sem.at[3], req_sem.at[4])
+    fields = jnp.where(part == 2, mark.astype(jnp.float32), fields)
+    fields = jnp.where(part == 3, turn.astype(jnp.float32), fields)
+    entry = jnp.where((there == z) & fits, chip * POOL + place, -1)
+    entry = jnp.where(guest & (seat < PASS), FIRST + (mark - 1) * PASS + seat, entry)
+    got = jnp.zeros((8, ENTRIES), jnp.float32)
+    for c in range(PLANES):
+        where_at = ones_where(iota((ENTRIES, toks), 0) == entry[8 * c : 8 * c + 1])
+        got = got + dot_nt(fields[8 * c : 8 * c + 8], where_at)
+    mark = got[2:3, :FIRST].astype(jnp.int32)
+    turn = got[3:4, :FIRST].astype(jnp.int32)
+    pass_at = jnp.where((mark > 0) & (turn < PASS), (mark - 1) * PASS + turn, -1)
+    taker = ones_where(iota((SPARE, FIRST), 0) == pass_at)
+    staying = (iota((1, ENTRIES), 1) >= FIRST) | (got[2:3] < 0.5)
+    entry_row = jnp.where(staying, got[0:1], 0.0)
+    entry_owner = got[1:2].astype(jnp.int32)
+    valid = entry_row > 0.0
+    entry_chip = jnp.where(valid, entry_owner >> 1, -1)
+    entry_core = (entry_owner & 1).astype(jnp.float32)
+    place_in = ranks(entry_chip, CHIPS, ENTRIES)
+    late = late + ones_where(jnp.max(place_in, axis=1, keepdims=True) >= PAIR)
+    fits_in = valid & (place_in < PAIR)
+    line = iota((CHIPS * 8, ENTRIES), 0)
+    part_in = line & 7
+    sent = jnp.where(part_in == 0, entry_row, jnp.where(part_in == 1, entry_core, 0.0))
+    sent = jnp.where((line >> 3) == entry_chip, sent, 0.0)
+    lanes = CHIPS // 2 * PAIR
+    lane_at = jnp.where(fits_in, lax.rem(p, CHIPS // 2) * PAIR + place_in, -1)
+    where_at = ones_where(iota((lanes, ENTRIES), 0) == lane_at)
+    message = dot_nt(sent, where_at) + jnp.where(iota((CHIPS * 8, lanes), 0) & 7 == 2, late, 0.0)
+    preq_send[...] = message.reshape(CHIPS, 8, lanes)
+    p_start(preq_send, preq_recv, req_sem.at[5], req_sem.at[6], req_sem.at[7])
+
+    slot = jnp.where(fits, there * POOL + place, -1)
+    slot = jnp.sum(jnp.where(iota(shape, 0) == z * 8, slot, 0).astype(jnp.float32), axis=0, keepdims=True)
+    packer = ones_where(iota((FIRST, toks), 0) == slot.astype(jnp.int32))
+    pack[...] = packer.astype(bf16)
 
     def store(ref, k, matrix, rows):
         for h in range(2):
@@ -273,47 +333,10 @@
         z_start(z_send.at[k], g1_recv.at[k], g1_sem.at[0, k], g1_sem.at[1, k], g1_sem.at[2, k], POOL // BLOCK)
 
 
-    wait_recv(zreq_recv, PLANES, req_sem.at[3], req_sem.at[4])
-    got = zreq_recv[...]
-    got = got.sum(axis=0)
-    late = jnp.sum(got[2:3], axis=1, keepdims=True)
-    mark = got[3:4].astype(jnp.int32)
-    turn = ranks(mark - 1, 2, FIRST)
-    late = late + ones_where(jnp.max(jnp.where(mark > 0, turn, 0), axis=1, keepdims=True) >= PASS)
-    pass_at = jnp.where((mark > 0) & (turn < PASS), (mark - 1) * PASS + turn, -1)
-    taker = ones_where(iota((SPARE, FIRST), 0) == pass_at)
-    take[...] = taker[: 2 * PASS].astype(bf16)
-    message = dot_nt(jnp.concatenate([got[0:2], jnp.zeros((6, FIRST), jnp.float32)], axis=0), taker)
-    lane = iota((8, LANE), 1)
-    onreq_send[0] = jnp.where(lane < PASS, message, 0.0)
-    onreq_send[1] = jnp.where(lane >= PASS, message, 0.0)
-    for side in range(2):
-        passed(onreq_send, onreq_recv, lambda i: onreq_sem.at[i], 0, side).start()
-    got = jnp.where(mark > 0, 0.0, got)
-    for side in range(2):
-        passed(onreq_send, onreq_recv, lambda i: onreq_sem.at[i], 0, side).wait()
-    got = jnp.concatenate([got, onreq_recv[0] + onreq_recv[1]], axis=1)
-    entry_row = got[0:1]
-    entry_owner = got[1:2].astype(jnp.int32)
-    valid = entry_row > 0.0
-    entry_chip = jnp.where(valid, entry_owner >> 1, -1)
-    entry_core = (entry_owner & 1).astype(jnp.float32)
-    place = ranks(entry_chip, CHIPS, ENTRIES)
-    late = late + ones_where(jnp.max(place, axis=1, keepdims=True) >= PAIR)
-    fits = valid & (place < PAIR)
-    line = iota((CHIPS * 8, ENTRIES), 0)
-    part = line & 7
-    fields = jnp.where(part == 0, entry_row, jnp.where(part == 1, entry_core, 0.0))
-    fields = jnp.where((line >> 3) == entry_chip, fields, 0.0)
-    lanes = CHIPS // 2 * PAIR
-    lane_at = jnp.where(fits, lax.rem(p, CHIPS // 2) * PAIR + place, -1)
-    where_at = ones_where(iota((lanes, ENTRIES), 0) == lane_at)
-    message = dot_nt(fields, where_at) + jnp.where(iota((CHIPS * 8, lanes), 0) & 7 == 2, late, 0.0)
-    preq_send[...] = message.reshape(CHIPS, 8, lanes)
-    p_start(preq_send, preq_recv, req_sem.at[5], req_sem.at[6], req_sem.at[7])
     pack_grads(0)
     unpack[...] = packer.T.astype(bf16)
-    spreader = ones_where(iota((SLOTS, ENTRIES), 0) == jnp.where(fits, entry_chip * PAIR + place, -1))
+    take[...] = taker[: 2 * PASS].astype(bf16)
+    spreader = ones_where(iota((SLOTS, ENTRIES), 0) == jnp.where(fits_in, entry_chip * PAIR + place_in, -1))
     spread[...] = spreader.astype(bf16)
     returned = [taker[PASS : 2 * PASS], taker[:PASS], taker[2 * PASS :]]
     unspread[...] = jnp.concatenate([spreader[:, :FIRST]] + returned, axis=0).T.astype(bf16)
@@ -434,7 +457,7 @@
         mate_out(tgr, tgr_hbm, 6, k).wait()
 
     loop(0, CHUNKS, drain)
-    wait_bytes(zreq_send, PLANES - 1, req_sem.at[2])
+    wait_bytes(line_recv, line_count - 1, req_sem.at[0])
     wait_bytes(preq_send, CHIPS - 1, req_sem.at[5])
     wait_bytes(flag_send, PLANES - 1, late_sem.at[0])
 
@@ -452,9 +475,7 @@
 
     row_block = pltpu.VMEM((CHUNKS, CORES, ROWS, width), bf16)
     tok_block = pltpu.VMEM((CHUNKS, CORES, TOKS, width), bf16)
-    z_note = pltpu.VMEM((PLANES, 8, FIRST), f32)
     late_note = pltpu.VMEM((PLANES, 8, LANE), f32)
-    on_note = pltpu.VMEM((2, 8, LANE), f32)
     p_note = pltpu.VMEM((CHIPS, 8, CHIPS // 2 * PAIR), f32)
     return pl.pallas_call(
         kernel,
@@ -470,9 +491,8 @@
             blocks(FIRST), blocks(ENTRIES), blocks(FIRST),
             blocks(SLOTS), blocks(SLOTS + SPARE), blocks(SLOTS),
             blocks(2 * PASS), blocks(2 * PASS),
-            pltpu.VMEM((8, TOKS), jnp.int32), pltpu.VMEM((CORES, 8, TOKS), jnp.int32),
-            z_note, z_note, p_note, p_note, late_note, late_note,
-            on_note, on_note,
+            pltpu.VMEM((8, TOKS), jnp.int32), pltpu.VMEM((PLANES * CORES, 8, TOKS), jnp.int32),
+            p_note, p_note, late_note, late_note,
             pltpu.VMEM((FIRST, toks), bf16),
             pltpu.VMEM((toks, FIRST), bf16),
             pltpu.VMEM((SLOTS, ENTRIES), bf16),
@@ -486,7 +506,6 @@
             dma((8, CHUNKS)),
             dma((3,)),
             dma((8,)),
-            dma((4,)),
             dma((3, CHUNKS)),
             dma((3, CHUNKS)),
             dma((3, CHUNKS)),

time: 177 us -> 175 us (0.989)
  Pallas kernels: 171 us -> 168 us
    pallas_call x1, Pallas kernels: 171 us -> 168 us  [routed(): pl.pallas_call(kernel, out_shape=(jax.ShapeDtypeStruct((TOKS, depth), bf1...]
where the time goes in v4:
time: 175 us; the launch traced here: 174 us
  Pallas kernels  168 us (96%)
  local copies, waits for them, and re-layouts  5.27 us (3%)
    pallas_call x1, Pallas kernels, routed(): pl.pallas_call(kernel, out_shape=(jax.ShapeDtypeStruct((TOKS, depth), bf1...  168 us
    unnamed x8, local copies, waits for them, and re-layouts  5.27 us

profile of v4, /device:TPU:1, one launch (start us, length us, event | category | flops | bytes accessed | tf_op | source)
XLA Modules:
  0.0 174.5 jit_solution(9659498215417518190)
XLA Ops:
  0.6 0.0 copy-start.2
  0.6 0.0 copy-start
  0.6 167.7 %shard_map.50 = (bf16[128,8192]{1,0:T(8,128)(2,1)}, bf16[256,8192]{1,0:T(8,128)(2,1)}, f32[1,1]{1,0:T(1,128)}) custom-call(s32[1,128]{1,0:T(1,128)} %bitcast.7, bf16[256,8192]{1,0:T(8,128)(2,1)} %table_hbm.1, bf16[128,8192]{1,0:T(8,128)(2,1)} %grads_hbm.1), custom_call_target="tpu_custom_call" | custom-call | tf_op jit(solution)/shard_map/pallas_call | solution.py:480
  168.4 0.0 copy-done.2
  168.4 0.0 copy-done
  168.4 0.8 while.11
  169.2 0.0 copy-start.1
  169.2 3.2 %copy.20 = bf16[128,8192]{1,0:T(8,128)(2,1)} copy(bf16[128,8192]{1,0:T(8,128)(2,1)} %get-tuple-element.80) | data formatting | bytes 4194304
  172.5 0.0 copy-done.1
  172.5 2.0 %copy.21 = bf16[256,8192]{1,0:T(8,128)(2,1)} copy(bf16[256,8192]{1,0:T(8,128)(2,1)S(1)} %copy-done.1) | data formatting | bytes 8388608
Async XLA Ops:
  0.6 167.8 %copy-start.2 = (s32[128]{0:T(128)S(1)}, s32[128]{0:T(128)}, u32[]{:S(2)}) copy-start(s32[128]{0:T(128)} %param.6) | copy-start | bytes 1540
  0.6 167.8 %copy-start = (bf16[128,8192]{1,0:T(8,128)(2,1)S(1)}, bf16[128,8192]{1,0:T(8,128)(2,1)}, u32[]{:S(2)}) copy-start(bf16[128,8192]{1,0:T(8,128)(2,1)} %grads_hbm.1) | copy-start | bytes 6291460
  169.2 3.3 %copy-start.1 = (bf16[256,8192]{1,0:T(8,128)(2,1)S(1)}, bf16[256,8192]{1,0:T(8,128)(2,1)}, u32[]{:S(2)}) copy-start(bf16[256,8192]{1,0:T(8,128)(2,1)} %get-tuple-element.81) | copy-start | bytes 12582916

commit v5 on v4

--- a/solution.py
+++ b/solution.py
@@ -134,6 +134,20 @@
     def columns(which, k):
         return pl.ds(pl.multiple_of((which * CHUNKS + k) * width, width), width)
 
+    barrier = pltpu.get_barrier_semaphore()
+
+    def greet(plane, chip, which):
+        pl.semaphore_signal(barrier, inc=1, device_id=device(plane, chip, which), device_id_type=MESH)
+
+    line_count = PLANES * CORES
+    line_me = z * CORES + core
+
+    def line_peer(j):
+        return lax.rem(line_me + j, line_count)
+
+    loop(1, line_count, lambda j: greet(line_peer(j) // CORES, p, lax.rem(line_peer(j), CORES)))
+    loop(1, CHIPS, lambda j: greet(z, p_peer(j), core))
+
     def own_in(hbm, vmem, i, k):
         return pltpu.make_async_copy(hbm.at[:, columns(core, k)], vmem.at[k, core], in_sem.at[i, k])
 
@@ -155,20 +169,6 @@
         e1_recv[k, pl.ds(first, count)] = jnp.zeros((count, BLOCK, width), bf16)
 
     loop(0, CHUNKS, clear)
-
-    barrier = pltpu.get_barrier_semaphore()
-
-    def greet(plane, chip, which):
-        pl.semaphore_signal(barrier, inc=1, device_id=device(plane, chip, which), device_id_type=MESH)
-
-    line_count = PLANES * CORES
-    line_me = z * CORES + core
-
-    def line_peer(j):
-        return lax.rem(line_me + j, line_count)
-
-    loop(1, line_count, lambda j: greet(line_peer(j) // CORES, p, lax.rem(line_peer(j), CORES)))
-    loop(1, CHIPS, lambda j: greet(z, p_peer(j), core))
 
     def z_start(src, dst, send, recv, own, count=1):
         def at(ref, t):
@@ -388,30 +388,16 @@
             back(k, side).start()
 
     def second_hop(k):
+        wait_bytes(p_send.at[k], (CHIPS - 1) * (PAIR // BLOCK), e1_sem.at[0, k])
+        for side in range(2):
+            on(k, side).wait_recv()
+        store(p_send, k, spread[...], g1_recv[k].reshape(ENTRIES, width))
+        p_start(p_send.at[k], g2_recv.at[k], g2_sem.at[0, k], g2_sem.at[1, k], g2_sem.at[2, k], PAIR // BLOCK)
         wait_bytes(z_send.at[k], (PLANES - 1) * (POOL // BLOCK), g1_sem.at[0, k])
         for side in range(2):
             back(k, side).wait_recv()
         store(z_send, k, unspread[...], e1_recv[k].reshape(SLOTS + SPARE, width))
         z_start(z_send.at[k], e2_recv.at[k], e2_sem.at[0, k], e2_sem.at[1, k], e2_sem.at[2, k], POOL // BLOCK)
-        wait_bytes(p_send.at[k], (CHIPS - 1) * (PAIR // BLOCK), e1_sem.at[0, k])
-        for side in range(2):
-            on(k, side).wait_recv()
-        store(p_send, k, spread[...], g1_recv[k].reshape(ENTRIES, width))
-        p_start(p_send.at[k], g2_recv.at[k], g2_sem.at[0, k], g2_sem.at[1, k], g2_sem.at[2, k], PAIR // BLOCK)
-
-    def turn_round(k):
-        pass_on(k)
-        second_hop(k - 1)
-
-    def whole_step(k):
-        turn_round(k)
-        first_hop(k + LEAD)
-
-    pass_on(0)
-    first_hop(LEAD)
-    loop(1, CHUNKS - LEAD, whole_step)
-    loop(CHUNKS - LEAD, CHUNKS, turn_round)
-    second_hop(CHUNKS - 1)
 
     def own_out(vmem, hbm, i, k):
         return pltpu.make_async_copy(vmem.at[k, core], hbm.at[:, columns(core, k)], out_sem.at[i, k])
@@ -439,7 +425,28 @@
         mate_out(tgr, tgr_hbm, 6, k).start()
         own_out(tgr, tgr_hbm, 1, k).start()
 
-    loop(0, CHUNKS, finish)
+    def turn_round(k):
+        pass_on(k)
+        second_hop(k - 1)
+
+    def whole_step(k):
+        turn_round(k)
+        first_hop(k + LEAD)
+
+    pass_on(0)
+    first_hop(LEAD)
+    loop(1, CHUNKS - LEAD, whole_step)
+    done = 2
+
+    def late_step(k):
+        turn_round(k)
+        finish(k - (CHUNKS - done))
+
+    loop(CHUNKS - LEAD, CHUNKS - done, turn_round)
+    loop(CHUNKS - done, CHUNKS, late_step)
+    second_hop(CHUNKS - 1)
+    loop(done, CHUNKS, finish)
+
     wait_recv(flag_recv, PLANES, late_sem.at[1], late_sem.at[2])
     flag_ref[0, 0] = jnp.max(flag_recv[...])
 

time: 175 us -> 174 us (level)
  no operation moved by 1% of the time
where the time goes in v5:
time: 174 us
  Pallas kernels  167 us (96%)
  local copies, waits for them, and re-layouts  5.27 us (3%)
    pallas_call x1, Pallas kernels, routed(): pl.pallas_call(kernel, out_shape=(jax.ShapeDtypeStruct((TOKS, depth), bf1...  167 us
    unnamed x8, local copies, waits for them, and re-layouts  5.27 us

profile of v5, /device:TPU:1, one launch (start us, length us, event | category | flops | bytes accessed | tf_op | source)
XLA Modules:
  0.0 174.1 jit_solution(9755589710117415417)
XLA Ops:
  0.6 0.0 copy-start.2
  0.6 0.0 copy-start
  0.6 167.4 %shard_map.50 = (bf16[128,8192]{1,0:T(8,128)(2,1)}, bf16[256,8192]{1,0:T(8,128)(2,1)}, f32[1,1]{1,0:T(1,128)}) custom-call(s32[1,128]{1,0:T(1,128)} %bitcast.7, bf16[256,8192]{1,0:T(8,128)(2,1)} %table_hbm.1, bf16[128,8192]{1,0:T(8,128)(2,1)} %grads_hbm.1), custom_call_target="tpu_custom_call" | custom-call | tf_op jit(solution)/shard_map/pallas_call | solution.py:487
  168.1 0.0 copy-done.2
  168.1 0.0 copy-done
  168.1 0.8 while.11
  168.9 0.0 copy-start.1
  168.9 3.2 %copy.20 = bf16[128,8192]{1,0:T(8,128)(2,1)} copy(bf16[128,8192]{1,0:T(8,128)(2,1)} %get-tuple-element.80) | data formatting | bytes 4194304
  172.1 0.0 copy-done.1
  172.1 2.0 %copy.21 = bf16[256,8192]{1,0:T(8,128)(2,1)} copy(bf16[256,8192]{1,0:T(8,128)(2,1)S(1)} %copy-done.1) | data formatting | bytes 8388608
Async XLA Ops:
  0.6 167.4 %copy-start.2 = (s32[128]{0:T(128)S(1)}, s32[128]{0:T(128)}, u32[]{:S(2)}) copy-start(s32[128]{0:T(128)} %param.6) | copy-start | bytes 1540
  0.6 167.4 %copy-start = (bf16[128,8192]{1,0:T(8,128)(2,1)S(1)}, bf16[128,8192]{1,0:T(8,128)(2,1)}, u32[]{:S(2)}) copy-start(bf16[128,8192]{1,0:T(8,128)(2,1)} %grads_hbm.1) | copy-start | bytes 6291460
  168.9 3.3 %copy-start.1 = (bf16[256,8192]{1,0:T(8,128)(2,1)S(1)}, bf16[256,8192]{1,0:T(8,128)(2,1)}, u32[]{:S(2)}) copy-start(bf16[256,8192]{1,0:T(8,128)(2,1)} %get-tuple-element.81) | copy-start | bytes 12582916
